TPU v7x, 32 devices: a whole 2x2x4 slice. The times are simulated.
32 devices in a mesh: gx: 4 (over y, core), gy: 8 (over z, x).
Axes of the slice: x: 2, y: 2, z: 4, core: 2. Of those that a mesh axis runs over, the one named last changes fastest.
Arguments:
- cell_state: float32 [16, 262144], P(None, ('gx', 'gy')), may hold values from -6 to 6
- geometry: float32 [7, 131072], P(None, ('gx', 'gy')), may hold values from -8 to 8, as said below
- surface_cell: int32 [131072], P(('gx', 'gy')), may hold values from 0 to 8191
- counts: int32 [32], P(('gx', 'gy')), may hold values from 32 to 4096, as said below
- wavenumbers: float32 [4], replicated, may hold values from 8 to 24
- target: float32 [4, 2, 2048], replicated, may hold values from -6 to 6
- direction_weight: float32 [2048], replicated, may hold values from 0.3 to 3
Outputs:
- far_field: float32 [4, 2, 2048], replicated
- objective: float32 [], replicated
- cell_adjoint: float32 [16, 262144], P(None, ('gx', 'gy'))
Inputs may be any that keep to these rules, and one draw needn't show every extreme that they name: Every count is a multiple of 32; one device's count is 4096; all counts together make 32 * 1024. `geometry`: rows 3 to 5 are unit vectors; row 6 is positive.
All inputs are finite; a program needn't handle non-finite values.
Results may differ from a plain program's by a relative error of at most 0.022.
Values sent between devices are 32-bit elements; how exact they have to be, the bound alone decides.
No kernel may reach another device: no remote copies, remote signals or barrier semaphores. Data moves between devices by JAX's collectives and lax.ppermute only.
A program may use at most 128 MiB of HBM per device.

v0:
```python
import math

import jax
import jax.numpy as jnp
from jax import lax
from jax.sharding import PartitionSpec as P

GOLDEN = math.pi * (3.0 - math.sqrt(5.0))


def directions(count_dirs):
    lattice = jnp.arange(count_dirs).astype(jnp.float32)
    height = 1.0 - (2.0 * lattice + 1.0) / count_dirs
    radius_xy = jnp.sqrt(1.0 - height * height)
    azimuth = jnp.mod(lattice * GOLDEN, 2.0 * math.pi)
    return (radius_xy * jnp.cos(azimuth), radius_xy * jnp.sin(azimuth), height)


def kernel_block(points, wavenum, east_x, north_y, upward):
    phases = wavenum * (
        points[0][:, None] * east_x[None, :]
        + points[1][:, None] * north_y[None, :]
        + points[2][:, None] * upward[None, :]
    )
    return jnp.concatenate([jnp.cos(phases), jnp.sin(phases)], axis=1).astype(jnp.bfloat16)


def source_rows(rows_block, level):
    surface_area = rows_block[22]
    normal = rows_block[19:22]
    pressure_real = rows_block[level] * surface_area
    pressure_imag = rows_block[4 + level] * surface_area
    return jnp.stack(
        [
            rows_block[8 + level] * surface_area,
            normal[0] * pressure_real,
            normal[1] * pressure_real,
            normal[2] * pressure_real,
            rows_block[12 + level] * surface_area,
            normal[0] * pressure_imag,
            normal[1] * pressure_imag,
            normal[2] * pressure_imag,
        ]
    ).astype(jnp.bfloat16)


def far_field_of(sums, wavenumbers, direction_basis):
    half_width = sums.shape[2] // 2
    cosine_part = sums[:, :, :half_width]
    sine_part = sums[:, :, half_width:]
    real_q = cosine_part[:, 0:4] + sine_part[:, 4:8]
    imag_q = cosine_part[:, 4:8] - sine_part[:, 0:4]
    real_z = jnp.sum(direction_basis[None] * real_q, axis=1)
    imag_z = jnp.sum(direction_basis[None] * imag_q, axis=1)
    wavenum = wavenumbers[:, None]
    return jnp.stack([-wavenum * imag_z, wavenum * real_z], axis=1)


def adjoint_weights(far_field, target, direction_weight, wavenumbers, direction_basis):
    count_dirs = far_field.shape[2]
    mismatch = far_field - target
    objective = jnp.sum(direction_weight * mismatch * mismatch) / count_dirs
    gradient = 2.0 * direction_weight * mismatch / count_dirs
    wavenum = wavenumbers[:, None]
    real_gz = wavenum * gradient[:, 1]
    imag_gz = -wavenum * gradient[:, 0]
    real_gq = direction_basis[None] * real_gz[:, None]
    imag_gq = direction_basis[None] * imag_gz[:, None]
    upper_half = jnp.concatenate([real_gq, -imag_gq], axis=2)
    lower_half = jnp.concatenate([imag_gq, real_gq], axis=2)
    return (objective, jnp.concatenate([upper_half, lower_half], axis=1).astype(jnp.bfloat16))


def adjoint_sources(products, normal):
    pressure_real = jnp.sum(normal[None] * products[:, 1:4], axis=1)
    pressure_imag = jnp.sum(normal[None] * products[:, 5:8], axis=1)
    return jnp.concatenate([pressure_real, pressure_imag, products[:, 0], products[:, 4]], axis=0)


def on_device(cell_state, geometry, surface_cell, counts, wavenumbers, target, direction_weight):
    owners = lax.axis_size(("gx", "gy"))
    rows_dev = surface_cell.shape[0]
    capacity = rows_dev // owners
    live_own = rows_dev // 4
    count_dirs = target.shape[2]
    num_freqs = wavenumbers.shape[0]
    living = (jnp.arange(rows_dev) < counts[0]).astype(jnp.float32)
    outgoing = (
        jnp.concatenate(
            [cell_state[:, surface_cell], geometry, jnp.ones((1, rows_dev), jnp.float32)], axis=0
        )
        * living[None, :]
    )
    outgoing = outgoing.reshape(24, capacity, owners)
    arrived = lax.all_to_all(outgoing, ("gx", "gy"), split_axis=2, concat_axis=2, tiled=True)
    marker = arrived[23]
    per_source = jnp.sum(marker, axis=0).astype(jnp.int32)
    offset = jnp.cumsum(per_source) - per_source
    position = offset[None, :] + jnp.arange(capacity, dtype=jnp.int32)[:, None]
    packed_slot = jnp.where(marker > 0.5, position, live_own).reshape(capacity * owners)
    compact = (
        jnp.zeros((23, live_own), jnp.float32)
        .at[:, packed_slot]
        .set(arrived[:23].reshape(23, capacity * owners), mode="drop")
    )
    block_rows = math.gcd(live_own, 1024)
    block_count = live_own // block_rows
    blocks = compact.reshape(23, block_count, block_rows).transpose(1, 0, 2)
    east_x, north_y, upward = directions(count_dirs)
    direction_basis = jnp.stack([jnp.ones_like(east_x), east_x, north_y, upward])

    def forward_block(running, rows_block):
        products = [
            jnp.dot(
                source_rows(rows_block, level),
                kernel_block(rows_block[16:19], wavenumbers[level], east_x, north_y, upward),
                preferred_element_type=jnp.float32,
            )
            for level in range(num_freqs)
        ]
        return (running + jnp.stack(products), None)

    sums, _ = lax.scan(
        forward_block, jnp.zeros((num_freqs, 8, 2 * count_dirs), jnp.float32), blocks
    )
    far_field = lax.psum(far_field_of(sums, wavenumbers, direction_basis), ("gx", "gy"))
    objective, weights = adjoint_weights(
        far_field, target, direction_weight, wavenumbers, direction_basis
    )

    def adjoint_block(carry, rows_block):
        products = [
            lax.dot_general(
                weights[level],
                kernel_block(rows_block[16:19], wavenumbers[level], east_x, north_y, upward),
                (((1,), (1,)), ((), ())),
                preferred_element_type=jnp.float32,
            )
            for level in range(num_freqs)
        ]
        return (carry, adjoint_sources(jnp.stack(products), rows_block[19:22]))

    _, backward = lax.scan(adjoint_block, jnp.zeros((), jnp.float32), blocks)
    backward = backward.transpose(1, 0, 2).reshape(16, live_own)
    spread = backward[:, jnp.minimum(packed_slot, live_own - 1)] * marker.reshape(
        1, capacity * owners
    )
    spread = spread.reshape(16, capacity, owners)
    returned = lax.all_to_all(spread, ("gx", "gy"), split_axis=2, concat_axis=2, tiled=True)
    per_row = returned.reshape(16, rows_dev) * living[None, :]
    cell_adjoint = jnp.zeros(cell_state.shape, jnp.float32).at[:, surface_cell].add(per_row)
    return (far_field, objective, cell_adjoint)


def solution(mesh):
    placed = (
        P(None, ("gx", "gy")),
        P(None, ("gx", "gy")),
        P(("gx", "gy")),
        P(("gx", "gy")),
        P(),
        P(),
        P(),
    )
    return jax.shard_map(
        on_device,
        mesh=mesh,
        in_specs=placed,
        out_specs=(P(), P(), P(None, ("gx", "gy"))),
        check_vma=False,
    )
```

profile of v0, /device:TPU:0, one launch (start us, length us, event | category | flops | bytes accessed | tf_op | source)
XLA Modules:
  0.0 432.0 jit_solution(11958232690904261717)
XLA Ops:
  9.8 3.5 copy.203
  13.3 13.0 %gather_fusion = f32[4096,16]{1,0:T(8,128)S(1)} fusion(f32[16,8192]{0,1:T(8,128)} %copy.203, s32[4096]{0:T(1024)S(1)} %get-tuple-element.113), kind=kCustom, calls=%fused_computation | custom fusion | bytes 540672 | tf_op jit(solution)/shard_map/gather | solution.py:90
  26.3 1.3 copy.204
  28.5 7.3 %all-to-all-start = ((f32[24,128,32]{1,0,2:T(8,128)}), f32[24,128,32]{1,0,2:T(8,128)S(1)}, u32[]{:S(2)}, u32[]{:S(2)}) async-start(f32[24,128,32]{1,0,2:T(8,128)} %maximum_multiply_fusion), calls=%async_computation | async-start | bytes 786432 | tf_op jit(solution)/shard_map/all_to_all | solution.py:95
  37.0 12.4 %all-to-all-done = f32[24,128,32]{1,0,2:T(8,128)S(1)} async-done(((f32[24,128,32]{1,0,2:T(8,128)}), f32[24,128,32]{1,0,2:T(8,128)S(1)}, u32[]{:S(2)}, u32[]{:S(2)}) %all-to-all-start) | async-done | bytes 393248 | tf_op jit(solution)/shard_map/all_to_all | solution.py:95
  52.0 10.7 %scatter_custom_fusion = f32[23,1024]{0,1:T(8,128)S(1)} fusion(s32[4096]{0:T(1024)S(1)} %bitcast.82, f32[4096,23]{1,0:T(8,128)S(1)} %copy.210, f32[]{:T(128)} %constant.23.clone.1), kind=kCustom, calls=%fused_computation.46 | custom fusion | bytes 94212 | tf_op jit(solution)/shard_map/scatter | solution.py:104
  62.8 1.4 slice_reduce_fusion.2
  64.2 5.4 %fusion.47 = (f32[1,1024]{0,1:T(8,128)}, f32[1,1024]{0,1:T(8,128)}, f32[1,1024]{0,1:T(8,128)}, f32[1,1024]{0,1:T(8,128)}, f32[1,1024]{0,1:T(8,128)}, /*index=5*/...) fusion(f32[23,1024]{0,1:T(8,128)S(1)} %scatter_custom_fusion), kind=kLoop, calls=%fused_computation.154 | loop fusion | bytes 155648 | tf_op jit(solution)/shard_map/while/body/eval_jaxpr/slice | solution.py:32
  89.4 126.5 %cosine_convert_fusion.3 = (bf16[1024,2048]{1,0:T(8,128)(2,1)S(1)}, bf16[1024,2048]{1,0:T(8,128)(2,1)}, bf16[1024,2048]{1,0:T(8,128)(2,1)}, bf16[1024,2048]{1,0:...) fusion(f32[2048]{0:T(1024)S(1)} %multiply_subtract_fusion, ...), kind=kLoop, calls=%fused_computation.15 | loop fusion | flops 35651584 | bytes 33591312 | tf_op jit(solution)/shard_map/convert.36
  217.8 1.3 copy-done.2
  219.2 4.1 fusion.14
  223.4 4.1 fusion.13
  227.6 4.3 fusion.15
  233.4 115.0 %all-reduce.2.cloned.1.call-done = f32[4,2,2048]{2,0,1:T(4,128)} async-done(((f32[4,2,2048]{2,0,1:T(4,128)}), f32[4,2,2048]{2,0,1:T(4,128)}) %all-reduce.2.cloned.1.call-update) | async-done | bytes 65552 | tf_op jit(solution)/shard_map/psum | solution.py:126
  348.4 1.5 multiply_multiply_fusion.1
  350.2 4.8 %fusion.21 = f32[1,8,1024]{2,1,0:T(8,128)S(1)} fusion(bf16[1024,2048]{1,0:T(8,128)(2,1)} %get-tuple-element.107, bf16[1024,2048]{1,0:T(8,128)(2,1)} %get-tuple-element.108, bf16[4,8,4096]{2,1,0:T(8,128)(2,1)S(1)} %maximum_maximum_fusion), kind=kOutput, calls=%fused_computation.38 | convolution fusion | flops 83886080 | bytes 8486912 | tf_op jit(solution)/shard_map/while/body/eval_jaxpr/dot_general | solution.py:133
  356.1 2.3 fusion.20
  359.6 2.3 fusion.19
  363.0 2.3 fusion.18
  365.7 10.8 %gather_fusion.1 = f32[4096,16]{1,0:T(8,128)S(1)} fusion(f32[16,1024]{0,1:T(8,128)S(1)} %copy.234, s32[4096]{0:T(1024)S(1)} %broadcast_clamp_fusion), kind=kCustom, calls=%fused_computation.1 | custom fusion | bytes 540672 | tf_op jit(solution)/shard_map/gather | solution.py:145
  378.5 5.6 %all-to-all-start.1 = ((f32[16,128,32]{1,0,2:T(8,128)}), f32[16,128,32]{1,0,2:T(8,128)S(1)}, u32[]{:S(2)}, u32[]{:S(2)}) async-start(f32[16,128,32]{1,0,2:T(8,128)} %broadcast_multiply_fusion), calls=%async_computation.1 | async-start | bytes 524288 | tf_op jit(solution)/shard_map/all_to_all | solution.py:149
  385.5 9.0 %all-to-all-done.1 = f32[16,128,32]{1,0,2:T(8,128)S(1)} async-done(((f32[16,128,32]{1,0,2:T(8,128)}), f32[16,128,32]{1,0,2:T(8,128)S(1)}, u32[]{:S(2)}, u32[]{:S(2)}) %all-to-all-start.1) | async-done | bytes 262176 | tf_op jit(solution)/shard_map/all_to_all | solution.py:149
  396.0 24.5 %scatter_custom_fusion.1 = f32[16,8192]{0,1:T(8,128)} fusion(s32[4096]{0:T(1024)S(1)} %get-tuple-element.112, f32[4096,16]{1,0:T(8,128)S(1)} %copy.237, f32[]{:T(128)} %constant.23.clone.1), kind=kCustom, calls=%fused_computation.33 | custom fusion | flops 65536 | bytes 524292 | tf_op jit(solution)/shard_map/scatter-add | solution.py:151
  420.5 3.5 copy.239
  (109 shorter events, 38.3 us)
Async XLA Ops:
  13.3 22.5 %copy-start.11 = (f32[4]{0:T(128)S(1)}, f32[4]{0:T(128)}, u32[]{:S(2)}) copy-start(f32[4]{0:T(128)} %param.11) | copy-start | bytes 52
  13.3 23.6 %copy-start.10 = (f32[2048]{0:T(1024)S(1)}, f32[2048]{0:T(1024)}, u32[]{:S(2)}) copy-start(f32[2048]{0:T(1024)} %param.13) | copy-start | bytes 24580
  28.5 20.8 %all-to-all-start = ((f32[24,128,32]{1,0,2:T(8,128)}), f32[24,128,32]{1,0,2:T(8,128)S(1)}, u32[]{:S(2)}, u32[]{:S(2)}) async-start(f32[24,128,32]{1,0,2:T(8,128)} %maximum_multiply_fusion), calls=%async_computation | async-start | bytes 786432 | tf_op jit(solution)/shard_map/all_to_all | solution.py:95
  35.8 312.6 %all-reduce.2.cloned.1.call-start = ((), (), s32[]{:S(2)}) async-start(), calls=%async_computation.2 | async-start | bytes 131072 | tf_op jit(solution)/shard_map/psum | solution.py:126
  215.8 1.9 copy-start
  215.8 3.3 copy-start.2
  227.6 120.8 %copy-start.9 = (f32[4,2,2048]{2,1,0:T(2,128)S(1)}, f32[4,2,2048]{2,1,0:T(2,128)}, u32[]{:S(2)}) copy-start(f32[4,2,2048]{2,1,0:T(2,128)} %param.12) | copy-start | bytes 196612
  350.2 4.8 %copy-start.6 = (bf16[1024,2048]{1,0:T(8,128)(2,1)S(1)}, bf16[1024,2048]{1,0:T(8,128)(2,1)}, u32[]{:S(2)}) copy-start(bf16[1024,2048]{1,0:T(8,128)(2,1)} %get-tuple-element.102) | copy-start | bytes 12582916
  350.2 5.9 %copy-start.7 = (bf16[1024,2048]{1,0:T(8,128)(2,1)S(1)}, bf16[1024,2048]{1,0:T(8,128)(2,1)}, u32[]{:S(2)}) copy-start(bf16[1024,2048]{1,0:T(8,128)(2,1)} %get-tuple-element.106) | copy-start | bytes 12582916
  356.1 2.3 copy-start.4
  356.1 3.5 copy-start.5
  359.6 2.3 copy-start.1
  359.6 3.5 copy-start.3
  365.3 19.5 %copy-start.8 = (f32[4,2,2048]{2,0,1:T(4,128)S(1)}, f32[4,2,2048]{2,0,1:T(4,128)}, u32[]{:S(2)}) copy-start(f32[4,2,2048]{2,0,1:T(4,128)} %all-reduce.2.cloned.1.call-done) | copy-start | bytes 196612
  378.5 16.0 %all-to-all-start.1 = ((f32[16,128,32]{1,0,2:T(8,128)}), f32[16,128,32]{1,0,2:T(8,128)S(1)}, u32[]{:S(2)}, u32[]{:S(2)}) async-start(f32[16,128,32]{1,0,2:T(8,128)} %broadcast_multiply_fusion), calls=%async_computation.1 | async-start | bytes 524288 | tf_op jit(solution)/shard_map/all_to_all | solution.py:149
Sparse Core Ops, SparseCore 0:
  233.1 115.2 all-reduce.1
where the time goes:
time: 433 us; the launch traced here: 432 us
  other arithmetic  157 us (36%)
  waiting for transfers between devices  136 us (31%)
  local copies, waits for them, and re-layouts  83.1 us (19%)
  matrix products  25.3 us (6%)
  between operations  16.9 us (4%)
  starting transfers between devices  13 us (3%)
    another operation x6, other arithmetic  127 us
    psum x1, waiting for transfers between devices, on_device(): lax.psum(far_field_of(sums, wavenumbers, direction_basis), ('gx', 'gy'))  115 us
    unnamed x49, local copies, waits for them, and re-layouts  32.8 us
    scatter-add x1, other arithmetic, on_device(): jnp.zeros(cell_state.shape, jnp.float32).at[:, surface_cell].add(per_row)  24.5 us
    dot_general x4, matrix products, forward_block(): jnp.dot(source_rows(rows_block, level), kernel_block(rows_block[16:19], w...  13.7 us
    gather x1, local copies, waits for them, and re-layouts, on_device(): cell_state[:, surface_cell]  13 us
    all_to_all x1, waiting for transfers between devices, on_device(): lax.all_to_all(outgoing, ('gx', 'gy'), split_axis=2, concat_axis=2, tiled...  12.4 us
    gather x2, local copies, waits for them, and re-layouts, on_device(): backward[:, jnp.minimum(packed_slot, live_own - 1)]  12 us
  transfers between devices with their start and end apart: 3, of which 3 were waited for; matrix products, arithmetic and copies ran while one was open for 0% of the time, Pallas kernels for 0%

commit v1 on v0

v1 whole, which is shorter than its diff:
```python
import functools
import math

import jax
import jax.numpy as jnp
import numpy as np
from jax import lax
from jax.experimental import pallas as pl
from jax.experimental.pallas import tpu as pltpu
from jax.sharding import PartitionSpec as P

GOLDEN = math.pi * (3.0 - math.sqrt(5.0))
AXES = ("gx", "gy")
F32 = jnp.float32
BF16 = jnp.bfloat16
LANES = 128
FREQS = 4
VMEM_BYTES = 48 * 2**20

SIN_K, SIN_A, SIN_B = 2.299546, 1.116939, 0.118212
COS_K, COS_A, COS_B = 3.583841, 0.682394, 0.186797


def direction_tables(count_dirs):
    lattice = np.arange(count_dirs).astype(np.float32)
    height = (np.float32(1.0) - (np.float32(2.0) * lattice + np.float32(1.0)) / np.float32(count_dirs)).astype(np.float32)
    radius_xy = np.sqrt(np.float32(1.0) - height * height).astype(np.float32)
    azimuth = np.mod(lattice * np.float32(GOLDEN), np.float32(2.0 * math.pi)).astype(np.float32)
    d = np.stack([radius_xy * np.cos(azimuth), radius_xy * np.sin(azimuth), height]).astype(np.float32)
    basis = np.concatenate([np.ones((1, count_dirs), np.float32), d, np.zeros((4, count_dirs), np.float32)])
    d1 = d.astype(jnp.bfloat16)
    d2 = (d - d1.astype(np.float32)).astype(jnp.bfloat16)
    d3 = (d - d1.astype(np.float32) - d2.astype(np.float32)).astype(jnp.bfloat16)
    parts = np.concatenate([d1, d1, d1, d2, d2, d3, d2, d3, np.zeros((8, count_dirs), d1.dtype)])
    return basis, np.concatenate([parts] * FREQS)


def bf16_parts(x):
    x1 = x.astype(BF16).astype(F32)
    x2 = (x - x1).astype(BF16).astype(F32)
    return x1, x2, x - x1 - x2


def gather_kernel(count_ref, cell_ref, rows_ref, out_ref, a1_ref, a2_ref, *, cap, owners, chunk):
    cells = cell_ref.shape[1]
    high = cells // 256
    for h in range(high):
        part = cell_ref[:, h * 256 : (h + 1) * 256]
        top = part.astype(BF16)
        a1_ref[h * 16 : (h + 1) * 16, :] = top
        a2_ref[h * 16 : (h + 1) * 16, :] = (part - top.astype(F32)).astype(BF16)
    live_slots = count_ref[0] // owners
    marker = live_slots.astype(F32)
    lane = lax.broadcasted_iota(jnp.int32, (1, LANES), 1)
    live = (lane % cap) < live_slots
    tiles = out_ref.shape[0]

    @pl.loop(0, tiles // chunk)
    def _(step):
        width = chunk * LANES
        base = step * chunk
        cell = jnp.concatenate([rows_ref[base + t, 7:8, :] for t in range(chunk)], axis=1)
        hi = jnp.floor(cell * (1.0 / 256.0))
        lo = cell - hi * 256.0
        level = lax.broadcasted_iota(jnp.int32, (256, width), 0).astype(F32)
        pick = jnp.where(level == lo, 1.0, 0.0).astype(BF16)
        found = jnp.dot(a1_ref[...], pick, preferred_element_type=F32) + jnp.dot(
            a2_ref[...], pick, preferred_element_type=F32
        )
        hi = jnp.broadcast_to(hi, (16, width))
        total = jnp.zeros((16, width), F32)
        for h in range(high):
            total = jnp.where(hi == float(h), found[h * 16 : (h + 1) * 16, :], total)
        for t in range(chunk):
            rows = rows_ref[base + t]
            out_ref[base + t, 0:16, :] = jnp.where(
                live, total[:, t * LANES : (t + 1) * LANES] * rows[6:7, :], 0.0
            )
            out_ref[base + t, 16:24, :] = jnp.where(live, rows, 0.0)
            out_ref[base + t, 23:24, :] = jnp.full((1, LANES), 1.0, F32) * marker


def forward_kernel(
    size_ref, start_ref, wave_ref, came_ref, parts_ref, basis_ref,
    t_ref, s_ref, far_ref, rows_ref, packed_ref, y_ref, src_ref,
):
    sources = came_ref.shape[0]
    live_own = rows_ref.shape[1]
    blocks = live_own // LANES
    width = far_ref.shape[1]

    @pl.when(pl.program_id(0) == 0)
    def _():
        packed_ref[...] = jnp.zeros(packed_ref.shape, F32)
        lane = lax.broadcasted_iota(jnp.int32, (24, LANES), 1)

        @pl.loop(0, sources)
        def _(s):
            offset = start_ref[s]
            base = offset // LANES
            shift = offset % LANES
            tile = jnp.where(lane < size_ref[s], came_ref[s], 0.0)
            tile = pltpu.roll(tile, shift, 1)
            packed_ref[base] += jnp.where(lane >= shift, tile, 0.0)
            packed_ref[base + 1] += jnp.where(lane >= shift, 0.0, tile)

        rows = jnp.concatenate([packed_ref[b] for b in range(blocks)], axis=1)
        rows_ref[...] = rows[16:24]
        point = rows[16:19]
        normal = rows[19:22]
        turned = []
        for f in range(FREQS):
            y1, y2, y3 = bf16_parts(point * (wave_ref[f] * (0.5 / math.pi)))
            turned += [y1, y2, y3, y1, y2, y1, y3, y2, jnp.zeros((8, live_own), F32)]
        turned = jnp.concatenate(turned, axis=0).T
        column = lax.broadcasted_iota(jnp.int32, (live_own, LANES), 1)
        for f in range(FREQS):
            mine = (column >= 32 * f) & (column < 32 * f + 32)
            y_ref[f] = jnp.where(mine, turned, 0.0).astype(BF16)
            real = jnp.concatenate([rows[8 + f : 9 + f], normal * rows[f : f + 1]], axis=0)
            imag = jnp.concatenate([rows[12 + f : 13 + f], normal * rows[4 + f : 5 + f]], axis=0)
            src_ref[f, 0] = jnp.concatenate([real, imag], axis=0).astype(BF16)
            src_ref[f, 1] = jnp.concatenate([imag, -real], axis=0).astype(BF16)

    piece = 256
    far = []
    for f in range(FREQS):
        total_t = jnp.zeros((8, width), F32)
        total_s = jnp.zeros((8, width), F32)
        for i in range(live_own // piece):
            at = slice(i * piece, (i + 1) * piece)
            turns = jnp.dot(y_ref[f, at, :], parts_ref[...], preferred_element_type=F32)
            t_val, s_val = half_angle(turns)
            t_ref[0, f, at, :] = t_val
            s_ref[0, f, at, :] = s_val
            total_t += jnp.dot(src_ref[f, 0, :, at], t_val, preferred_element_type=F32)
            total_s += jnp.dot(src_ref[f, 1, :, at], s_val, preferred_element_type=F32)
        whole = jnp.sum(src_ref[f, 0].astype(F32), axis=1, keepdims=True)
        q = whole - (2.0 * SIN_K * SIN_K) * total_t + (2.0 * SIN_K * COS_K) * total_s
        weighted = q * jnp.concatenate([basis_ref[0:4, :]] * 2, axis=0)
        real_z = jnp.sum(weighted[0:4], axis=0, keepdims=True)
        imag_z = jnp.sum(weighted[4:8], axis=0, keepdims=True)
        far += [imag_z * (-wave_ref[f]), real_z * wave_ref[f]]
    far_ref[...] = jnp.concatenate(far, axis=0)


def half_angle(turns):
    r = turns - jnp.round(turns)
    u = r * r
    v = u - SIN_A
    half_sin = (v * v + SIN_B) * r
    w = u - COS_A
    half_cos = w * w - COS_B
    return (half_sin * half_sin).astype(BF16), (half_sin * half_cos).astype(BF16)


def adjoint_kernel(
    size_ref, start_ref, wave_ref, far_ref, target_ref, weight_ref, basis_ref, rows_ref, t_ref, s_ref,
    out_ref, cost_ref, sum_ref, acc_ref, flat_ref, *, count_dirs,
):
    step = pl.program_id(0)
    live_own = rows_ref.shape[1]
    blocks = live_own // LANES
    mismatch = far_ref[...] - target_ref[...]
    weight = weight_ref[...]
    pull = weight * mismatch
    cost = pull * mismatch
    gradient = pull * (2.0 / count_dirs)
    basis = jnp.concatenate([basis_ref[0:4, :]] * 2, axis=0)

    @pl.when(step == 0)
    def _():
        acc_ref[...] = jnp.zeros(acc_ref.shape, F32)
        sum_ref[...] = jnp.zeros(sum_ref.shape, F32)

    sum_ref[...] += cost
    contract = (((1,), (1,)), ((), ()))
    for f in range(FREQS):
        real_gz = gradient[2 * f + 1 : 2 * f + 2] * wave_ref[f]
        imag_gz = gradient[2 * f : 2 * f + 1] * (-wave_ref[f])
        four = (4, real_gz.shape[1])
        real_gz = jnp.broadcast_to(real_gz, four)
        imag_gz = jnp.broadcast_to(imag_gz, four)
        for_cos = (basis * jnp.concatenate([real_gz, imag_gz], axis=0)).astype(BF16)
        for_sin = (basis * jnp.concatenate([-imag_gz, real_gz], axis=0)).astype(BF16)
        whole = jnp.sum(for_cos.astype(F32), axis=1, keepdims=True)
        part = lax.dot_general(for_cos, t_ref[0, f], contract, preferred_element_type=F32)
        other = lax.dot_general(for_sin, s_ref[0, f], contract, preferred_element_type=F32)
        acc_ref[f] += whole - (2.0 * SIN_K * SIN_K) * part + (2.0 * SIN_K * COS_K) * other

    @pl.when(step == pl.num_programs(0) - 1)
    def _():
        cost_ref[0] = jnp.sum(sum_ref[...]) / count_dirs
        normal = rows_ref[3:6]
        pressure_real, pressure_imag, velocity_real, velocity_imag = [], [], [], []
        for f in range(FREQS):
            got = acc_ref[f]
            pressure_real.append(jnp.sum(normal * got[1:4], axis=0, keepdims=True))
            pressure_imag.append(jnp.sum(normal * got[5:8], axis=0, keepdims=True))
            velocity_real.append(got[0:1])
            velocity_imag.append(got[4:5])
        flat = jnp.concatenate(pressure_real + pressure_imag + velocity_real + velocity_imag, axis=0)
        for b in range(blocks):
            flat_ref[b] = flat[:, b * LANES : (b + 1) * LANES]
        flat_ref[blocks] = jnp.zeros((16, LANES), F32)
        lane = lax.broadcasted_iota(jnp.int32, (16, LANES), 1)

        @pl.loop(0, out_ref.shape[0])
        def _(s):
            offset = start_ref[s]
            base = offset // LANES
            shift = offset % LANES
            back = (LANES - shift) % LANES
            first = pltpu.roll(flat_ref[base], back, 1)
            second = pltpu.roll(flat_ref[base + 1], back, 1)
            joined = jnp.where(lane < LANES - shift, first, second)
            out_ref[s] = jnp.where(lane < size_ref[s], joined, 0.0)


def scatter_kernel(value_ref, rows_ref, out_ref, *, chunk):
    tiles = value_ref.shape[0]
    high = out_ref.shape[1] // 256
    width = chunk * LANES
    contract = (((1,), (1,)), ((), ()))

    def body(step, total):
        base = step * chunk
        cell = jnp.concatenate([rows_ref[base + t, 7:8, :] for t in range(chunk)], axis=1)
        value = jnp.concatenate([value_ref[base + t] for t in range(chunk)], axis=1)
        hi = jnp.floor(cell * (1.0 / 256.0))
        lo = cell - hi * 256.0
        level = lax.broadcasted_iota(jnp.int32, (256, width), 0).astype(F32)
        pick = jnp.where(level == lo, 1.0, 0.0).astype(BF16)
        top = value.astype(BF16)
        rest = (value - top.astype(F32)).astype(BF16)
        hi = jnp.broadcast_to(hi, (16, width)).astype(BF16)
        zero = jnp.zeros((16, width), BF16)
        tops = jnp.concatenate([jnp.where(hi == float(h), top, zero) for h in range(high)], axis=0)
        rests = jnp.concatenate([jnp.where(hi == float(h), rest, zero) for h in range(high)], axis=0)
        total = total + lax.dot_general(tops, pick, contract, preferred_element_type=F32)
        return total + lax.dot_general(rests, pick, contract, preferred_element_type=F32)

    total = lax.fori_loop(0, tiles // chunk, body, jnp.zeros((high * 16, 256), F32))
    for h in range(high):
        out_ref[:, h * 256 : (h + 1) * 256] = total[h * 16 : (h + 1) * 16, :]


def smem():
    return pl.BlockSpec(memory_space=pltpu.SMEM)


def params():
    return pltpu.CompilerParams(vmem_limit_bytes=VMEM_BYTES)


def to_tiles(x, cap):
    owners, channels, _ = x.shape
    if cap == LANES:
        return x
    many = LANES // cap
    x = x.reshape(owners // many, many, channels, cap).transpose(0, 2, 1, 3)
    return x.reshape(owners // many, channels, LANES)


def from_tiles(x, cap):
    tiles, channels, _ = x.shape
    if cap == LANES:
        return x
    many = LANES // cap
    x = x.reshape(tiles, channels, many, cap).transpose(0, 2, 1, 3)
    return x.reshape(tiles * many, channels, cap)


def all_sum(x):
    for axis in AXES:
        size = lax.axis_size(axis)
        hop = 1
        while hop < size:
            x = x + lax.ppermute(x, axis, [(i, i ^ hop) for i in range(size)])
            hop *= 2
    return x


def on_device(cell_state, geometry, surface_cell, counts, wavenumbers, target, direction_weight):
    owners = lax.axis_size(AXES)
    rows_dev = surface_cell.shape[0]
    cells = cell_state.shape[1]
    cap = rows_dev // owners
    live_own = rows_dev // 4
    count_dirs = target.shape[2]
    tiles = rows_dev // LANES
    high = cells // 256
    basis, parts = direction_tables(count_dirs)
    basis, parts = jnp.asarray(basis), jnp.asarray(parts)

    rows = jnp.concatenate([geometry, surface_cell.astype(F32)[None, :]], axis=0)
    rows = to_tiles(rows.reshape(8, cap, owners).transpose(2, 0, 1), cap)
    outgoing = pl.pallas_call(
        functools.partial(gather_kernel, cap=cap, owners=owners, chunk=4),
        in_specs=[smem(), pl.BlockSpec(memory_space=pltpu.VMEM), pl.BlockSpec(memory_space=pltpu.VMEM)],
        out_shape=jax.ShapeDtypeStruct((tiles, 24, LANES), F32),
        scratch_shapes=[pltpu.VMEM((high * 16, 256), BF16), pltpu.VMEM((high * 16, 256), BF16)],
        compiler_params=params(),
        name="gather_rows",
    )(counts, cell_state, rows)
    outgoing = from_tiles(outgoing, cap)
    came = lax.all_to_all(outgoing, AXES, split_axis=0, concat_axis=0, tiled=True)
    size = came[:, 23, 0].astype(jnp.int32)
    start = jnp.cumsum(size) - size
    if cap < LANES:
        came = jnp.pad(came, ((0, 0), (0, 0), (0, LANES - cap)))

    width = 256
    grid = count_dirs // width
    block = pl.BlockSpec((1, FREQS, live_own, width), lambda i: (i, 0, 0, 0))
    stored = jax.ShapeDtypeStruct((grid, FREQS, live_own, width), BF16)
    by_dir = lambda i: (0, i)
    whole2 = lambda i: (0, 0)
    t_all, s_all, far, kept = pl.pallas_call(
        forward_kernel,
        grid=(grid,),
        in_specs=[
            smem(), smem(), smem(),
            pl.BlockSpec((owners, 24, LANES), lambda i: (0, 0, 0)),
            pl.BlockSpec((32 * FREQS, width), by_dir),
            pl.BlockSpec((8, width), by_dir),
        ],
        out_specs=[block, block, pl.BlockSpec((2 * FREQS, width), by_dir), pl.BlockSpec((8, live_own), whole2)],
        out_shape=[
            stored, stored,
            jax.ShapeDtypeStruct((2 * FREQS, count_dirs), F32),
            jax.ShapeDtypeStruct((8, live_own), F32),
        ],
        scratch_shapes=[
            pltpu.VMEM((live_own // LANES + 1, 24, LANES), F32),
            pltpu.VMEM((FREQS, live_own, LANES), BF16),
            pltpu.VMEM((FREQS, 2, 8, live_own), BF16),
        ],
        compiler_params=params(),
        name="forward",
    )(size, start, wavenumbers, came, parts, basis)

    far = all_sum(far)

    back, objective = pl.pallas_call(
        functools.partial(adjoint_kernel, count_dirs=count_dirs),
        grid=(grid,),
        in_specs=[
            smem(), smem(), smem(),
            pl.BlockSpec((2 * FREQS, width), by_dir),
            pl.BlockSpec((2 * FREQS, width), by_dir),
            pl.BlockSpec((1, width), by_dir),
            pl.BlockSpec((8, width), by_dir),
            pl.BlockSpec((8, live_own), whole2),
            block, block,
        ],
        out_specs=[pl.BlockSpec((owners, 16, LANES), lambda i: (0, 0, 0)), smem()],
        out_shape=[jax.ShapeDtypeStruct((owners, 16, LANES), F32), jax.ShapeDtypeStruct((1,), F32)],
        scratch_shapes=[
            pltpu.VMEM((2 * FREQS, width), F32),
            pltpu.VMEM((FREQS, 8, live_own), F32),
            pltpu.VMEM((live_own // LANES + 1, 16, LANES), F32),
        ],
        compiler_params=params(),
        name="adjoint",
    )(
        size, start, wavenumbers, far, target.reshape(2 * FREQS, count_dirs),
        direction_weight.reshape(1, count_dirs), basis, kept, t_all, s_all,
    )
    returned = lax.all_to_all(back[:, :, :cap], AXES, split_axis=0, concat_axis=0, tiled=True)
    cell_adjoint = pl.pallas_call(
        functools.partial(scatter_kernel, chunk=4),
        in_specs=[pl.BlockSpec(memory_space=pltpu.VMEM), pl.BlockSpec(memory_space=pltpu.VMEM)],
        out_shape=jax.ShapeDtypeStruct(cell_state.shape, F32),
        compiler_params=params(),
        name="scatter_rows",
    )(to_tiles(returned, cap), rows)
    return (far.reshape(FREQS, 2, count_dirs), objective[0], cell_adjoint)


def solution(mesh):
    placed = (
        P(None, AXES),
        P(None, AXES),
        P(AXES),
        P(AXES),
        P(),
        P(),
        P(),
    )
    return jax.shard_map(
        on_device,
        mesh=mesh,
        in_specs=placed,
        out_specs=(P(), P(), P(None, AXES)),
        check_vma=False,
    )
```

time: 433 us -> 128 us (0.30)
  other arithmetic: 157 us -> 1.66 us
  waiting for transfers between devices: 136 us -> 26.7 us
  local copies, waits for them, and re-layouts: 83.1 us -> 8.69 us
  Pallas kernels: 0 us -> 62.7 us
  matrix products: 25.3 us -> 0 us
  blocking collectives: 0 us -> 20.6 us
  between operations: 16.9 us -> 1.43 us
  starting transfers between devices: 13 us -> 5.11 us
    another operation x10 -> x2, other arithmetic: 128 us -> 0.17 us
    psum x1 -> x0, waiting for transfers between devices: 115 us -> none  [on_device(): lax.psum(far_field_of(sums, wavenumbers, direction_basis), ('gx', 'gy'))]
    pallas_call x0 -> x4, Pallas kernels: none -> 62.7 us  [the longest x1 35.1 us: on_device(): pl.pallas_call(forward_kernel, grid=(grid,), in_specs=[smem(), smem(), sm...]
    unnamed x49 -> x14, local copies, waits for them, and re-layouts: 32.8 us -> 5.76 us
    dot_general x8 -> x0, matrix products: 25.3 us -> none  [the longest x4 13.7 us: forward_block(): jnp.dot(source_rows(rows_block, level), kernel_block(rows_block[16:19], w...]
    gather x3 -> x0, local copies, waits for them, and re-layouts: 25 us -> none  [the longest x1 13 us: on_device(): cell_state[:, surface_cell]]
    scatter-add x1 -> x0, other arithmetic: 24.5 us -> none  [on_device(): jnp.zeros(cell_state.shape, jnp.float32).at[:, surface_cell].add(per_row)]
    all_to_all x0 -> x1, blocking collectives: none -> 20.6 us  [on_device(): lax.all_to_all(outgoing, AXES, split_axis=0, concat_axis=0, tiled=True)]
  transfers between devices with their start and end apart: 3 -> 6, of which waited for: 3 -> 6; matrix products, arithmetic and copies ran while one was open for 0% -> 1% of each run, Pallas kernels for 0% -> 0%
where the time goes in v1:
time: 128 us; the launch traced here: 127 us
  Pallas kernels  62.7 us (49%)
  waiting for transfers between devices  26.7 us (21%)
  blocking collectives  20.6 us (16%)
  local copies, waits for them, and re-layouts  8.69 us (7%)
  starting transfers between devices  5.11 us (4%)
  other arithmetic  1.66 us (1%)
  between operations  1.43 us (1%)
    pallas_call x1, Pallas kernels, on_device(): pl.pallas_call(forward_kernel, grid=(grid,), in_specs=[smem(), smem(), sm...  35.1 us
    all_to_all x1, blocking collectives, on_device(): lax.all_to_all(outgoing, AXES, split_axis=0, concat_axis=0, tiled=True)  20.6 us
    pallas_call x1, Pallas kernels, on_device(): pl.pallas_call(functools.partial(adjoint_kernel, count_dirs=count_dirs),...  18.9 us
    ppermute x5, waiting for transfers between devices, all_sum(): x = x + lax.ppermute(x, axis, [(i, i ^ hop) for i in range(size)])  16.8 us
    all_to_all x1, waiting for transfers between devices, on_device(): lax.all_to_all(back[:, :, :cap], AXES, split_axis=0, concat_axis=0, tiled...  9.97 us
    unnamed x14, local copies, waits for them, and re-layouts  5.76 us
    pallas_call x1, Pallas kernels, on_device(): pl.pallas_call(functools.partial(scatter_kernel, chunk=4), in_specs=[pl.B...  4.98 us
    pallas_call x1, Pallas kernels, on_device(): pl.pallas_call(functools.partial(gather_kernel, cap=cap, owners=owners, c...  3.69 us
  transfers between devices with their start and end apart: 6, of which 6 were waited for; matrix products, arithmetic and copies ran while one was open for 1% of the time, Pallas kernels for 0%

profile of v1, /device:TPU:0, one launch (start us, length us, event | category | flops | bytes accessed | tf_op | source)
XLA Modules:
  0.0 127.0 jit_solution(16671353967492671051)
XLA Ops:
  0.6 1.1 concatenate.8
  1.9 0.7 convert_element_type.10
  3.5 1.0 copy-done.1
  4.5 3.7 %gather_rows.1 = f32[32,24,128]{2,1,0:T(8,128)S(1)} custom-call(s32[1]{0:T(128)S(6)} %copy.16.count_ref, f32[16,8192]{1,0:T(8,128)S(1)} %copy-done.1, f32[32,8,128]{2,1,0:T(8,128)S(1)} %maximum_bitcast_fusion.rows_ref), custom_call_target="tpu_custom_call" | custom-call | tf_op jit(solution)/shard_map/gather_rows/pallas_call | solution.py:298
  8.2 20.6 %all_to_all.10.came_ref = f32[32,24,128]{2,1,0:T(8,128)S(1)} all-to-all(f32[32,24,128]{2,1,0:T(8,128)S(1)} %gather_rows.1), channel_id=1, replica_groups=mesh['gx'=4,'gy'=8] {'gx','gy'}, dimensions={0} | all-to-all | bytes 786432 | tf_op jit(solution)/shard_map/all_to_all | solution.py:307
  29.0 0.7 fusion.size_ref
  29.7 1.0 copy-done
  30.8 0.8 copy-done.2
  32.3 35.1 %forward.1 = (bf16[8,4,1024,256]{3,2,1,0:T(8,128)(2,1)}, bf16[8,4,1024,256]{3,2,1,0:T(8,128)(2,1)}, f32[8,2048]{1,0:T(8,128)S(1)}, f32[8,1024]{1,0:T(8,128)S(1)}) custom-call(s32[32]{0:T(128)S(1)} %fusion.size_ref, s32[32]{0:T(128)S(1)} %sub.3.start_ref, f32[4]{0:T(128)S(1)} %copy-done.5, f32[32,24,128]{2,1,0:T(8,128)S(1)} %all_to_all.10.came_ref, ...), custom_call_target="tpu_custom_call" | custom-call | tf_op jit(solution)/shard_map/forward/pallas_call | solution.py:319
  67.4 1.3 collective-permute-done
  69.3 3.7 %collective-permute-done.1 = f32[8,2048]{1,0:T(8,128)S(1)} collective-permute-done((f32[8,2048]{1,0:T(8,128)S(1)}, f32[8,2048]{1,0:T(8,128)S(1)}, u32[]{:S(2)}, u32[]{:S(2)}) %collective-permute-start.1) | collective-permute-done | bytes 65568 | tf_op jit(solution)/shard_map/ppermute | solution.py:279
  73.0 1.0 collective-permute-start.2
  74.0 3.4 %collective-permute-done.2 = f32[8,2048]{1,0:T(8,128)S(1)} collective-permute-done((f32[8,2048]{1,0:T(8,128)S(1)}, f32[8,2048]{1,0:T(8,128)S(1)}, u32[]{:S(2)}, u32[]{:S(2)}) %collective-permute-start.2) | collective-permute-done | bytes 65568 | tf_op jit(solution)/shard_map/ppermute | solution.py:279
  77.3 0.9 collective-permute-start.3
  78.2 3.5 %collective-permute-done.3 = f32[8,2048]{1,0:T(8,128)S(1)} collective-permute-done((f32[8,2048]{1,0:T(8,128)S(1)}, f32[8,2048]{1,0:T(8,128)S(1)}, u32[]{:S(2)}, u32[]{:S(2)}) %collective-permute-start.3) | collective-permute-done | bytes 65568 | tf_op jit(solution)/shard_map/ppermute | solution.py:279
  81.8 0.9 reshape.53.target_ref
  82.7 5.0 %collective-permute-done.4 = f32[8,2048]{1,0:T(8,128)S(1)} collective-permute-done((f32[8,2048]{1,0:T(8,128)S(1)}, f32[8,2048]{1,0:T(8,128)S(1)}, u32[]{:S(2)}, u32[]{:S(2)}) %collective-permute-start.4) | collective-permute-done | bytes 65568 | tf_op jit(solution)/shard_map/ppermute | solution.py:279
  87.6 0.8 copy-done.3
  88.5 0.7 copy-done.4
  89.8 18.9 %adjoint.1 = (f32[32,16,128]{2,1,0:T(8,128)}, f32[1]{0:T(128)}) custom-call(s32[32]{0:T(128)S(1)} %fusion.size_ref, s32[32]{0:T(128)S(1)} %sub.3.start_ref, f32[4]{0:T(128)S(1)} %copy-done.6, f32[8,2048]{1,0:T(8,128)S(1)} %add.19.far_ref, f32[8,2048]{1,0:T(8,128)S(1)} %reshape.53.target_ref, f32[1,2048]{1,0:T(1,128)S(1)} %bitcast.5, ...), custom_call_target="tpu_custom_call" | custom-call | tf_op jit(solution)/shard_map/adjoint/pallas_call | solution.py:345
  108.7 2.6 %all-to-all-start.1 = ((f32[32,16,128]{2,1,0:T(8,128)}), f32[32,16,128]{2,1,0:T(8,128)S(1)}, u32[]{:S(2)}, u32[]{:S(2)}) async-start(f32[32,16,128]{2,1,0:T(8,128)} %get-tuple-element.14), calls=%async_computation.1 | async-start | bytes 524288 | tf_op jit(solution)/shard_map/all_to_all | solution.py:370
  111.4 0.7 reshape.52
  112.0 10.0 %all-to-all-done.1.value_ref = f32[32,16,128]{2,1,0:T(8,128)S(1)} async-done(((f32[32,16,128]{2,1,0:T(8,128)}), f32[32,16,128]{2,1,0:T(8,128)S(1)}, u32[]{:S(2)}, u32[]{:S(2)}) %all-to-all-start.1) | async-done | bytes 262176 | tf_op jit(solution)/shard_map/all_to_all | solution.py:370
  122.0 5.0 %scatter_rows.1 = f32[16,8192]{1,0:T(8,128)} custom-call(f32[32,16,128]{2,1,0:T(8,128)S(1)} %all-to-all-done.1.value_ref, f32[32,8,128]{2,1,0:T(8,128)S(1)} %maximum_bitcast_fusion.rows_ref), custom_call_target="tpu_custom_call" | custom-call | tf_op jit(solution)/shard_map/scatter_rows/pallas_call | solution.py:371
  (25 shorter events, 2.6 us)
Async XLA Ops:
  3.5 1.0 copy-start.1
  29.7 1.0 copy-start
  30.8 0.8 copy-start.2
  31.6 0.7 copy-start.5
  67.4 1.3 collective-permute-start
  68.7 4.3 %collective-permute-start.1 = (f32[8,2048]{1,0:T(8,128)S(1)}, f32[8,2048]{1,0:T(8,128)S(1)}, u32[]{:S(2)}, u32[]{:S(2)}) collective-permute-start(f32[8,2048]{1,0:T(8,128)S(1)} %add.15), channel_id=1, source_target_pairs={{0,16},{8,24},{16,0},{24,8},{1,17},{9,25},{17,1},{25,9},{2,18},{10... | collective-permute-start | bytes 196616 | tf_op jit(solution)/shard_map/ppermute | solution.py:279
  73.0 4.3 %collective-permute-start.2 = (f32[8,2048]{1,0:T(8,128)S(1)}, f32[8,2048]{1,0:T(8,128)S(1)}, u32[]{:S(2)}, u32[]{:S(2)}) collective-permute-start(f32[8,2048]{1,0:T(8,128)S(1)} %add.16), channel_id=1, source_target_pairs={{0,1},{1,0},{2,3},{3,2},{4,5},{5,4},{6,7},{7,6},{8,9},{9,8},{10,11... | collective-permute-start | bytes 196616 | tf_op jit(solution)/shard_map/ppermute | solution.py:279
  77.3 4.3 %collective-permute-start.3 = (f32[8,2048]{1,0:T(8,128)S(1)}, f32[8,2048]{1,0:T(8,128)S(1)}, u32[]{:S(2)}, u32[]{:S(2)}) collective-permute-start(f32[8,2048]{1,0:T(8,128)S(1)} %add.17), channel_id=1, source_target_pairs={{0,2},{1,3},{2,0},{3,1},{4,6},{5,7},{6,4},{7,5},{8,10},{9,11},{10,... | collective-permute-start | bytes 196616 | tf_op jit(solution)/shard_map/ppermute | solution.py:279
  81.7 5.9 %collective-permute-start.4 = (f32[8,2048]{1,0:T(8,128)S(1)}, f32[8,2048]{1,0:T(8,128)S(1)}, u32[]{:S(2)}, u32[]{:S(2)}) collective-permute-start(f32[8,2048]{1,0:T(8,128)S(1)} %add.18), channel_id=1, source_target_pairs={{0,4},{1,5},{2,6},{3,7},{4,0},{5,1},{6,2},{7,3},{8,12},{9,13},{10,... | collective-permute-start | bytes 196616 | tf_op jit(solution)/shard_map/ppermute | solution.py:279
  87.6 0.8 copy-start.3
  88.5 0.7 copy-start.4
  89.2 0.7 copy-start.6
  108.7 13.3 %all-to-all-start.1 = ((f32[32,16,128]{2,1,0:T(8,128)}), f32[32,16,128]{2,1,0:T(8,128)S(1)}, u32[]{:S(2)}, u32[]{:S(2)}) async-start(f32[32,16,128]{2,1,0:T(8,128)} %get-tuple-element.14), calls=%async_computation.1 | async-start | bytes 524288 | tf_op jit(solution)/shard_map/all_to_all | solution.py:370

commit v2 on v1

v2 whole, which is shorter than its diff:
```python
import functools
import math

import jax
import jax.numpy as jnp
import numpy as np
from jax import lax
from jax.experimental import pallas as pl
from jax.experimental.pallas import tpu as pltpu
from jax.sharding import PartitionSpec as P

GOLDEN = math.pi * (3.0 - math.sqrt(5.0))
AXES = ("gx", "gy")
F32 = jnp.float32
BF16 = jnp.bfloat16
LANES = 128
FREQS = 4
VMEM_BYTES = 24 * 2**20
PIECE = 1024

SIN_K, SIN_A, SIN_B = 2.299546, 1.116939, 0.118212
COS_K, COS_A, COS_B = 3.583841, 0.682394, 0.186797
COS_SCALE = 2.0 * SIN_K * SIN_K
SIN_SCALE = 2.0 * SIN_K * COS_K


def direction_tables(count_dirs):
    lattice = np.arange(count_dirs).astype(np.float32)
    height = (np.float32(1.0) - (np.float32(2.0) * lattice + np.float32(1.0)) / np.float32(count_dirs)).astype(np.float32)
    radius_xy = np.sqrt(np.float32(1.0) - height * height).astype(np.float32)
    azimuth = np.mod(lattice * np.float32(GOLDEN), np.float32(2.0 * math.pi)).astype(np.float32)
    d = np.stack([radius_xy * np.cos(azimuth), radius_xy * np.sin(azimuth), height]).astype(np.float32)
    basis = np.concatenate([np.ones((1, count_dirs), np.float32), d, np.zeros((4, count_dirs), np.float32)])
    d1 = d.astype(jnp.bfloat16)
    d2 = (d - d1.astype(np.float32)).astype(jnp.bfloat16)
    d3 = (d - d1.astype(np.float32) - d2.astype(np.float32)).astype(jnp.bfloat16)
    parts = np.concatenate([d1, d1, d1, d2, d2, d3, d2, d3, np.zeros((8, count_dirs), d1.dtype)])
    return basis, np.concatenate([parts] * FREQS)


def bf16_parts(x):
    x1 = x.astype(BF16).astype(F32)
    x2 = (x - x1).astype(BF16).astype(F32)
    return x1, x2, x - x1 - x2


def gather_kernel(cell_ref, index_ref, rows_ref, out_ref, a1_ref, a2_ref, *, chunk):
    cells = cell_ref.shape[1]
    high = cells // 256
    for h in range(high):
        part = cell_ref[:, h * 256 : (h + 1) * 256]
        top = part.astype(BF16)
        a1_ref[h * 16 : (h + 1) * 16, :] = top
        a2_ref[h * 16 : (h + 1) * 16, :] = (part - top.astype(F32)).astype(BF16)
    tiles = out_ref.shape[0]

    @pl.loop(0, tiles // chunk)
    def _(step):
        width = chunk * LANES
        base = step * chunk
        cell = jnp.concatenate([index_ref[base + t] for t in range(chunk)], axis=1)
        hi = lax.shift_right_logical(cell, 8)
        lo = cell & 255
        level = lax.broadcasted_iota(jnp.int32, (256, width), 0)
        pick = jnp.where(level == lo, 1.0, 0.0).astype(BF16)
        found = jnp.dot(a1_ref[...], pick, preferred_element_type=F32) + jnp.dot(
            a2_ref[...], pick, preferred_element_type=F32
        )
        hi = jnp.broadcast_to(hi, (16, width))
        total = jnp.zeros((16, width), F32)
        for h in range(high):
            total = jnp.where(hi == h, found[h * 16 : (h + 1) * 16, :], total)
        for t in range(chunk):
            out_ref[base + t] = total[:, t * LANES : (t + 1) * LANES] * rows_ref[base + t, 6:7, :]


def pack_rows(ends_ref, came_ref, packed_ref):
    sources, channels, _ = came_ref.shape
    lane = lax.broadcasted_iota(jnp.int32, (channels, LANES), 1)

    def body(s, carry):
        offset = ends_ref[0, s]
        base = offset // LANES
        shift = offset % LANES
        tile = pltpu.roll(came_ref[s], shift, 1)
        pltpu.store(packed_ref.at[base], tile, mask=lane >= shift)
        pltpu.store(packed_ref.at[base + 1], tile, mask=lane < shift)
        return carry

    lax.fori_loop(0, sources, body, 0, unroll=8)
    return jnp.concatenate([packed_ref[b] for b in range(packed_ref.shape[0] - 1)], axis=1)


def half_angle(turns):
    r = turns - jnp.round(turns)
    u = r * r
    v = u - SIN_A
    half_sin = (v * v + SIN_B) * r
    w = u - COS_A
    half_cos = w * w - COS_B
    return (half_sin * half_sin).astype(BF16), (half_sin * half_cos).astype(BF16)


def masked_parts(parts_ref, f):
    parts = parts_ref[...]
    level = lax.broadcasted_iota(jnp.int32, parts.shape, 0)
    return jnp.where((level >= 32 * f) & (level < 32 * f + 32), parts.astype(F32), 0.0).astype(BF16)


def phase_kernel(ends_ref, wave_ref, came_ref, parts_ref, t_ref, s_ref, rows_ref, y_ref, packed_ref):
    live_own = rows_ref.shape[1]

    @pl.when(pl.program_id(0) == 0)
    def _():
        rows = pack_rows(ends_ref, came_ref, packed_ref)
        rows_ref[...] = rows
        turned = []
        for f in range(FREQS):
            y1, y2, y3 = bf16_parts(rows[0:3] * (wave_ref[f] * (0.5 / math.pi)))
            turned += [y1, y2, y3, y1, y2, y1, y3, y2, jnp.zeros((8, live_own), F32)]
        y_ref[...] = jnp.concatenate(turned, axis=0).T.astype(BF16)

    for f in range(FREQS):
        parts = masked_parts(parts_ref, f)
        for i in range(live_own // PIECE):
            at = slice(i * PIECE, (i + 1) * PIECE)
            turns = jnp.dot(y_ref[at, :], parts, preferred_element_type=F32)
            t_ref[0, f, at, :], s_ref[0, f, at, :] = half_angle(turns)


def radiate_kernel(
    ends_ref, wave_ref, came_ref, rows_ref, y_ref, parts_ref, basis_ref, first_t_ref, first_s_ref,
    far_ref, t_ref, s_ref, packed_ref, src_ref, t_sem, s_sem,
):
    live_own = rows_ref.shape[1]
    step = pl.program_id(0)
    steps = pl.num_programs(0)
    half, _, _, width = first_t_ref.shape

    def fetch(i):
        return (
            pltpu.make_async_copy(first_t_ref.at[i], t_ref.at[i], t_sem.at[i]),
            pltpu.make_async_copy(first_s_ref.at[i], s_ref.at[i], s_sem.at[i]),
        )

    @pl.when(step == 0)
    def _():
        for i in range(half):
            for copy in fetch(i):
                copy.start()
        rows = pack_rows(ends_ref, came_ref, packed_ref)
        normal = rows_ref[3:6]
        for f in range(FREQS):
            real = jnp.concatenate([rows[8 + f : 9 + f], normal * rows[f : f + 1]], axis=0)
            imag = jnp.concatenate([rows[12 + f : 13 + f], normal * rows[4 + f : 5 + f]], axis=0)
            src_ref[f, 0] = jnp.concatenate([real, imag], axis=0).astype(BF16)
            src_ref[f, 1] = jnp.concatenate([imag, -real], axis=0).astype(BF16)

    def project(f, total_t, total_s, basis):
        whole = jnp.sum(src_ref[f, 0].astype(F32), axis=1, keepdims=True)
        q = whole - COS_SCALE * total_t + SIN_SCALE * total_s
        weighted = q * jnp.concatenate([basis] * 2, axis=0)
        real_z = jnp.sum(weighted[0:4], axis=0, keepdims=True)
        imag_z = jnp.sum(weighted[4:8], axis=0, keepdims=True)
        return [imag_z * (-wave_ref[f]), real_z * wave_ref[f]]

    first, second = (pl.ds(pl.multiple_of(i * width, width), width) for i in (step, steps + step))
    basis1 = basis_ref[0:4, first]
    basis2 = basis_ref[0:4, second]
    far1, far2 = [], []
    for copy in fetch(step):
        copy.wait()
    for f in range(FREQS):
        total_t = jnp.dot(src_ref[f, 0], t_ref[step, f], preferred_element_type=F32)
        total_s = jnp.dot(src_ref[f, 1], s_ref[step, f], preferred_element_type=F32)
        far1 += project(f, total_t, total_s, basis1)
        parts = masked_parts(parts_ref, f)
        for i in range(live_own // PIECE):
            at = slice(i * PIECE, (i + 1) * PIECE)
            turns = jnp.dot(y_ref[at, :], parts, preferred_element_type=F32)
            t_ref[steps + step, f, at, :], s_ref[steps + step, f, at, :] = half_angle(turns)
        total_t = jnp.dot(src_ref[f, 0], t_ref[steps + step, f], preferred_element_type=F32)
        total_s = jnp.dot(src_ref[f, 1], s_ref[steps + step, f], preferred_element_type=F32)
        far2 += project(f, total_t, total_s, basis2)
    far_ref[:, first] = jnp.concatenate(far1, axis=0)
    far_ref[:, second] = jnp.concatenate(far2, axis=0)


def adjoint_kernel(
    ends_ref, wave_ref, far_ref, target_ref, weight_ref, basis_ref, rows_ref,
    t_ref, s_ref, out_ref, cost_ref, _t, _s, flat_ref,
):
    live_own = rows_ref.shape[1]
    blocks = live_own // LANES
    count_dirs = far_ref.shape[1]
    width = t_ref.shape[3]
    mismatch = far_ref[...] - jnp.concatenate([target_ref[f] for f in range(FREQS)], axis=0)
    pull = weight_ref[...] * mismatch
    cost_ref[0] = jnp.sum(pull * mismatch) / count_dirs
    gradient = pull * (2.0 / count_dirs)
    basis = jnp.concatenate([basis_ref[0:4, :]] * 2, axis=0)
    contract = (((1,), (1,)), ((), ()))
    normal = rows_ref[3:6]
    pressure_real, pressure_imag, velocity_real, velocity_imag = [], [], [], []
    for f in range(FREQS):
        real_gz = jnp.broadcast_to(gradient[2 * f + 1 : 2 * f + 2] * wave_ref[f], (4, count_dirs))
        imag_gz = jnp.broadcast_to(gradient[2 * f : 2 * f + 1] * (-wave_ref[f]), (4, count_dirs))
        for_cos = (basis * jnp.concatenate([real_gz, imag_gz], axis=0)).astype(BF16)
        for_sin = (basis * jnp.concatenate([-imag_gz, real_gz], axis=0)).astype(BF16)
        whole = jnp.sum(for_cos.astype(F32), axis=1, keepdims=True)
        total_t = jnp.zeros((8, live_own), F32)
        total_s = jnp.zeros((8, live_own), F32)
        for i in range(t_ref.shape[0]):
            at = slice(i * width, (i + 1) * width)
            total_t += lax.dot_general(for_cos[:, at], t_ref[i, f], contract, preferred_element_type=F32)
            total_s += lax.dot_general(for_sin[:, at], s_ref[i, f], contract, preferred_element_type=F32)
        got = whole - COS_SCALE * total_t + SIN_SCALE * total_s
        pressure_real.append(jnp.sum(normal * got[1:4], axis=0, keepdims=True))
        pressure_imag.append(jnp.sum(normal * got[5:8], axis=0, keepdims=True))
        velocity_real.append(got[0:1])
        velocity_imag.append(got[4:5])
    flat = jnp.concatenate(pressure_real + pressure_imag + velocity_real + velocity_imag, axis=0)
    for b in range(blocks):
        flat_ref[b] = flat[:, b * LANES : (b + 1) * LANES]
    flat_ref[blocks] = jnp.zeros((16, LANES), F32)
    lane = lax.broadcasted_iota(jnp.int32, (16, LANES), 1)

    def body(s, carry):
        offset = ends_ref[0, s]
        base = offset // LANES
        shift = offset % LANES
        back = (LANES - shift) % LANES
        joined = jnp.where(lane >= shift, flat_ref[base], flat_ref[base + 1])
        joined = pltpu.roll(joined, back, 1)
        out_ref[s] = jnp.where(lane < ends_ref[1, s], joined, 0.0)
        return carry

    lax.fori_loop(0, out_ref.shape[0], body, 0, unroll=8)


def scatter_kernel(value_ref, index_ref, out_ref, *, chunk):
    tiles = value_ref.shape[0]
    high = out_ref.shape[1] // 256
    width = chunk * LANES
    contract = (((1,), (1,)), ((), ()))

    def body(step, total):
        base = step * chunk
        cell = jnp.concatenate([index_ref[base + t] for t in range(chunk)], axis=1)
        value = jnp.concatenate([value_ref[base + t] for t in range(chunk)], axis=1)
        hi = lax.shift_right_logical(cell, 8)
        lo = cell & 255
        level = lax.broadcasted_iota(jnp.int32, (256, width), 0)
        pick = jnp.where(level == lo, 1.0, 0.0).astype(BF16)
        top = value.astype(BF16)
        rest = (value - top.astype(F32)).astype(BF16)
        hi = jnp.broadcast_to(hi, (16, width)).astype(F32).astype(BF16)
        zero = jnp.zeros((16, width), BF16)
        tops = jnp.concatenate([jnp.where(hi == float(h), top, zero) for h in range(high)], axis=0)
        rests = jnp.concatenate([jnp.where(hi == float(h), rest, zero) for h in range(high)], axis=0)
        total = total + lax.dot_general(tops, pick, contract, preferred_element_type=F32)
        return total + lax.dot_general(rests, pick, contract, preferred_element_type=F32)

    total = lax.fori_loop(0, tiles // chunk, body, jnp.zeros((high * 16, 256), F32))
    for h in range(high):
        out_ref[:, h * 256 : (h + 1) * 256] = total[h * 16 : (h + 1) * 16, :]


def smem():
    return pl.BlockSpec(memory_space=pltpu.SMEM)


def params():
    return pltpu.CompilerParams(vmem_limit_bytes=VMEM_BYTES)


def to_tiles(x, cap):
    owners, channels, _ = x.shape
    if cap == LANES:
        return x
    many = LANES // cap
    x = x.reshape(owners // many, many, channels, cap).transpose(0, 2, 1, 3)
    return x.reshape(owners // many, channels, LANES)


def from_tiles(x, cap):
    tiles, channels, _ = x.shape
    if cap == LANES:
        return x
    many = LANES // cap
    x = x.reshape(tiles, channels, many, cap).transpose(0, 2, 1, 3)
    return x.reshape(tiles * many, channels, cap)


def all_sum(x):
    gx, gy = (lax.axis_size(axis) for axis in AXES)
    low = gy.bit_length() - 1
    rest = [b for b in range((gx * gy).bit_length() - 1) if b != low]
    rounds = [[low]]
    if low % 2:
        rounds.append([rest.pop(0), rest.pop(-1)])
    rounds += [rest[i : i + 2] for i in range(0, len(rest), 2)]
    for bits in rounds:
        masks = [sum(1 << b for k, b in enumerate(bits) if code >> k & 1) for code in range(1, 1 << len(bits))]
        came = [lax.ppermute(x, AXES, [(i, i ^ m) for i in range(gx * gy)]) for m in masks]
        if len(came) == 1:
            x = x + came[0]
        else:
            x = (x + came[0]) + (came[1] + came[2])
    return x


def on_device(cell_state, geometry, surface_cell, counts, wavenumbers, target, direction_weight):
    owners = lax.axis_size(AXES)
    rows_dev = surface_cell.shape[0]
    cells = cell_state.shape[1]
    cap = rows_dev // owners
    live_own = rows_dev // 4
    count_dirs = target.shape[2]
    tiles = rows_dev // LANES
    high = cells // 256
    basis, parts = direction_tables(count_dirs)
    basis, parts = jnp.asarray(basis), jnp.asarray(parts)
    vmem = pl.BlockSpec(memory_space=pltpu.VMEM)

    share = (counts // owners).astype(F32)
    rows = jnp.concatenate([geometry, jnp.broadcast_to(share[None, :], (1, rows_dev))], axis=0)
    rows = rows.reshape(8, cap, owners).transpose(2, 0, 1)
    came = lax.all_to_all(rows, AXES, split_axis=0, concat_axis=0, tiled=True)
    index = to_tiles(surface_cell.reshape(cap, owners).T.reshape(owners, 1, cap), cap)
    outgoing = pl.pallas_call(
        functools.partial(gather_kernel, chunk=4),
        in_specs=[vmem, vmem, vmem],
        out_shape=jax.ShapeDtypeStruct((tiles, 16, LANES), F32),
        scratch_shapes=[pltpu.VMEM((high * 16, 256), BF16), pltpu.VMEM((high * 16, 256), BF16)],
        compiler_params=params(),
        name="gather_rows",
    )(cell_state, index, to_tiles(rows, cap))
    values = lax.all_to_all(from_tiles(outgoing, cap), AXES, split_axis=0, concat_axis=0, tiled=True)
    marks = np.stack([np.tril(np.ones((owners, owners), np.float32), -1), np.eye(owners, dtype=np.float32)])
    ends = jnp.sum(came[:, 7, 0] * marks, axis=2).astype(jnp.int32)
    if cap < LANES:
        came = jnp.pad(came, ((0, 0), (0, 0), (0, LANES - cap)))
        values = jnp.pad(values, ((0, 0), (0, 0), (0, LANES - cap)))

    parts, basis, came, values = (pltpu.with_memory_space_constraint(x, pltpu.HBM) for x in (parts, basis, came, values))
    width = 256
    half = count_dirs // width // 2
    packs = live_own // LANES + 1
    first = pltpu.HBM((half, FREQS, live_own, width), BF16)
    held = pltpu.VMEM((2 * half, FREQS, live_own, width), BF16)
    by_dir = lambda i: (0, i)
    block = pl.BlockSpec((1, FREQS, live_own, width), lambda i: (i, 0, 0, 0))
    first_t, first_s, kept, turned = pl.pallas_call(
        phase_kernel,
        grid=(half,),
        in_specs=[smem(), smem(), vmem, pl.BlockSpec((32 * FREQS, width), by_dir)],
        out_specs=[block, block, vmem, vmem],
        out_shape=[
            first, first,
            pltpu.HBM((8, live_own), F32),
            pltpu.HBM((live_own, 32 * FREQS), BF16),
        ],
        scratch_shapes=[pltpu.VMEM((packs, 8, LANES), F32)],
        compiler_params=params(),
        name="phases",
    )(ends, wavenumbers, came, parts)

    hbm = pl.BlockSpec(memory_space=pltpu.HBM)
    far, t_all, s_all = pl.pallas_call(
        radiate_kernel,
        grid=(half,),
        in_specs=[
            smem(), smem(), vmem, vmem, vmem,
            pl.BlockSpec((32 * FREQS, width), lambda i: (0, half + i)),
            vmem, hbm, hbm,
        ],
        out_specs=[vmem] * 3,
        out_shape=[jax.ShapeDtypeStruct((2 * FREQS, count_dirs), F32), held, held],
        scratch_shapes=[
            pltpu.VMEM((packs, 16, LANES), F32),
            pltpu.VMEM((FREQS, 2, 8, live_own), BF16),
            pltpu.SemaphoreType.DMA((half,)),
            pltpu.SemaphoreType.DMA((half,)),
        ],
        compiler_params=params(),
        name="radiate",
    )(ends, wavenumbers, values, kept, turned, parts, basis, first_t, first_s)

    far = all_sum(far)

    back, objective = pl.pallas_call(
        adjoint_kernel,
        in_specs=[smem(), smem()] + [vmem] * 7,
        out_specs=[vmem, smem(), vmem, vmem],
        out_shape=[
            jax.ShapeDtypeStruct((owners, 16, LANES), F32),
            jax.ShapeDtypeStruct((1,), F32),
            held, held,
        ],
        input_output_aliases={7: 2, 8: 3},
        scratch_shapes=[pltpu.VMEM((packs, 16, LANES), F32)],
        compiler_params=params(),
        name="adjoint",
    )(
        ends, wavenumbers, far, target, direction_weight.reshape(1, count_dirs), basis, kept, t_all, s_all,
    )[:2]
    returned = lax.all_to_all(back[:, :, :cap], AXES, split_axis=0, concat_axis=0, tiled=True)
    cell_adjoint = pl.pallas_call(
        functools.partial(scatter_kernel, chunk=4),
        in_specs=[vmem, vmem],
        out_shape=jax.ShapeDtypeStruct(cell_state.shape, F32),
        compiler_params=params(),
        name="scatter_rows",
    )(to_tiles(returned, cap), index)
    return (far.reshape(FREQS, 2, count_dirs), objective[0], cell_adjoint)


def solution(mesh):
    placed = (
        P(None, AXES),
        P(None, AXES),
        P(AXES),
        P(AXES),
        P(),
        P(),
        P(),
    )
    return jax.shard_map(
        on_device,
        mesh=mesh,
        in_specs=placed,
        out_specs=(P(), P(), P(None, AXES)),
        check_vma=False,
    )
```

time: 128 us -> 104 us (0.81)
  blocking collectives: 20.6 us -> 0 us
  starting transfers between devices: 5.11 us -> 23.6 us
  Pallas kernels: 62.7 us -> 47.2 us
  waiting for transfers between devices: 26.7 us -> 22.1 us
  local copies, waits for them, and re-layouts: 8.69 us -> 6.19 us
    all_to_all x1 -> x0, blocking collectives: 20.6 us -> none  [on_device(): lax.all_to_all(outgoing, AXES, split_axis=0, concat_axis=0, tiled=True)]
    pallas_call x4 -> x5, Pallas kernels: 62.7 us -> 47.2 us  [the longest x1 14.7 us: on_device(): pl.pallas_call(radiate_kernel, grid=(half,), in_specs=[smem(), smem(), vm...]
    all_to_all x0 -> x2, starting transfers between devices: none -> 12.7 us  [the longest x1 7.3 us: on_device(): came = lax.all_to_all(rows, AXES, split_axis=0, concat_axis=0, tiled=True)]
    ppermute x5 -> x7, starting transfers between devices: 2.5 us -> 8.31 us  [all_sum(): lax.ppermute(x, AXES, [(i, i ^ m) for i in range(gx * gy)])]
    ppermute x5 -> x7, waiting for transfers between devices: 16.8 us -> 11.7 us  [all_sum(): lax.ppermute(x, AXES, [(i, i ^ m) for i in range(gx * gy)])]
    unnamed x14 -> x12, local copies, waits for them, and re-layouts: 5.76 us -> 2.42 us
    add x5 -> x3, other arithmetic: 0.05 us -> 1.51 us  [the longest x1 0.85 us: all_sum(): x = x + came[0]]
    convert_element_type x3 -> x1, other arithmetic: 1.41 us -> 0.01 us  [on_device(): ends = jnp.sum(came[:, 7, 0] * marks, axis=2).astype(jnp.int32)]
  transfers between devices with their start and end apart: 6 -> 10, of which waited for: 6 -> 8; matrix products, arithmetic and copies ran while one was open for 1% -> 3% of each run, Pallas kernels for 0% -> 16%
where the time goes in v2:
time: 104 us; the launch traced here: 103 us
  Pallas kernels  47.2 us (45%)
  starting transfers between devices  23.6 us (23%)
  waiting for transfers between devices  22.1 us (21%)
  local copies, waits for them, and re-layouts  6.19 us (6%)
  other arithmetic  2.36 us (2%)
  between operations  1.4 us (1%)
    pallas_call x1, Pallas kernels, on_device(): pl.pallas_call(radiate_kernel, grid=(half,), in_specs=[smem(), smem(), vm...  14.7 us
    ppermute x7, waiting for transfers between devices, all_sum(): lax.ppermute(x, AXES, [(i, i ^ m) for i in range(gx * gy)])  11.7 us
    pallas_call x1, Pallas kernels, on_device(): pl.pallas_call(phase_kernel, grid=(half,), in_specs=[smem(), smem(), vmem...  11.3 us
    pallas_call x1, Pallas kernels, on_device(): pl.pallas_call(adjoint_kernel, in_specs=[smem(), smem()] + [vmem] * 7, ou...  10.9 us
    all_to_all x1, waiting for transfers between devices, on_device(): lax.all_to_all(back[:, :, :cap], AXES, split_axis=0, concat_axis=0, tiled...  9.96 us
    ppermute x7, starting transfers between devices, all_sum(): lax.ppermute(x, AXES, [(i, i ^ m) for i in range(gx * gy)])  8.31 us
    all_to_all x1, starting transfers between devices, on_device(): came = lax.all_to_all(rows, AXES, split_axis=0, concat_axis=0, tiled=True)  7.3 us
    all_to_all x1, starting transfers between devices, on_device(): lax.all_to_all(from_tiles(outgoing, cap), AXES, split_axis=0, concat_axis...  5.39 us
  transfers between devices with their start and end apart: 10, of which 8 were waited for; matrix products, arithmetic and copies ran while one was open for 3% of the time, Pallas kernels for 16%

profile of v2, /device:TPU:0, one launch (start us, length us, event | category | flops | bytes accessed | tf_op | source)
XLA Modules:
  0.0 102.9 jit_solution(13806582942574201170)
XLA Ops:
  1.3 0.9 concatenate.3
  2.4 0.8 copy.17
  3.2 7.3 %all-to-all-start = ((f32[32,8,128]{2,1,0:T(8,128)}), f32[32,8,128]{2,1,0:T(8,128)S(1)}, u32[]{:S(2)}, u32[]{:S(2)}) async-start(f32[32,8,128]{2,1,0:T(8,128)} %bitcast.1.rows_ref), calls=%async_computation | async-start | bytes 262144 | tf_op jit(solution)/shard_map/all_to_all | solution.py:329
  10.5 0.8 reshape.30
  11.4 1.1 %copy-done = f32[16,8192]{1,0:T(8,128)S(1)} copy-done((f32[16,8192]{1,0:T(8,128)S(1)}, f32[16,8192]{1,0:T(8,128)}, u32[]{:S(2)}) %copy-start) | copy-done | bytes 524312
  12.4 5.4 %gather_rows.1 = f32[32,16,128]{2,1,0:T(8,128)} custom-call(f32[16,8192]{1,0:T(8,128)S(1)} %copy-done, s32[32,1,128]{2,1,0:T(1,128)S(1)} %bitcast.7, f32[32,8,128]{2,1,0:T(8,128)} %bitcast.1.rows_ref), custom_call_target="tpu_custom_call" | custom-call | tf_op jit(solution)/shard_map/gather_rows/pallas_call | solution.py:331
  18.3 5.4 %all-to-all-start.1 = ((f32[32,16,128]{2,1,0:T(8,128)}), f32[32,16,128]{2,1,0:T(8,128)S(1)}, u32[]{:S(2)}, u32[]{:S(2)}) async-start(f32[32,16,128]{2,1,0:T(8,128)} %gather_rows.1), calls=%async_computation.1 | async-start | bytes 524288 | tf_op jit(solution)/shard_map/all_to_all | solution.py:339
  24.0 0.8 multiply_reduce_fusion
  25.5 11.3 %phases.1 = (bf16[4,4,1024,256]{3,2,1,0:T(8,128)(2,1)}, bf16[4,4,1024,256]{3,2,1,0:T(8,128)(2,1)}, f32[8,1024]{1,0:T(8,128)}, bf16[1024,128]{1,0:T(8,128)(2,1)}) custom-call(s32[2,32]{1,0:T(2,128)S(1)} %convert_element_type.7.ends_ref, f32[4]{0:T(128)S(1)} %copy-done.2, f32[32,8,128]{2,1,0:T(8,128)} %copy-done.4, bf16[128,2048]{1,0:T(8,128)(2,1)} %constant.31.clone.parts_ref), custom_call_target="tpu_custom_call" | custom-call | tf_op jit(solution)/shard_map/phases/pallas_call | solution.py:354
  37.5 14.7 %radiate.1 = (f32[8,2048]{1,0:T(8,128)}, bf16[8,4,1024,256]{3,2,1,0:T(8,128)(2,1)S(1)}, bf16[8,4,1024,256]{3,2,1,0:T(8,128)(2,1)S(1)}) custom-call(s32[2,32]{1,0:T(2,128)} %copy-done.1, f32[4]{0:T(128)} %wave_ref.5, f32[32,16,128]{2,1,0:T(8,128)} %copy-done.3, f32[8,1024]{1,0:T(8,128)} %get-tuple-element.12.rows_ref, ...), custom_call_target="tpu_custom_call" | custom-call | tf_op jit(solution)/shard_map/radiate/pallas_call | solution.py:370
  52.5 1.2 %collective-permute-done = f32[8,2048]{1,0:T(8,128)S(1)} collective-permute-done((f32[8,2048]{1,0:T(8,128)}, f32[8,2048]{1,0:T(8,128)S(1)}, u32[]{:S(2)}, u32[]{:S(2)}) %collective-permute-start) | collective-permute-done | bytes 65568 | tf_op jit(solution)/shard_map/ppermute | solution.py:305
  53.7 0.9 add.24
  54.6 1.8 %collective-permute-start.1 = (f32[8,2048]{1,0:T(8,128)S(1)}, f32[8,2048]{1,0:T(8,128)S(1)}, u32[]{:S(2)}, u32[]{:S(2)}) collective-permute-start(f32[8,2048]{1,0:T(8,128)S(1)} %add.24), channel_id=1, source_target_pairs={{0,1},{1,0},{2,3},{3,2},{4,5},{5,4},{6,7},{7,6},{8,9},{9,8},{10,11... | collective-permute-start | bytes 196616 | tf_op jit(solution)/shard_map/ppermute | solution.py:305
  56.4 1.5 %collective-permute-start.2 = (f32[8,2048]{1,0:T(8,128)S(1)}, f32[8,2048]{1,0:T(8,128)S(1)}, u32[]{:S(2)}, u32[]{:S(2)}) collective-permute-start(f32[8,2048]{1,0:T(8,128)S(1)} %add.24), channel_id=1, source_target_pairs={{0,16},{1,17},{2,18},{3,19},{4,20},{5,21},{6,22},{7,23},{8,24},{9,... | collective-permute-start | bytes 196616 | tf_op jit(solution)/shard_map/ppermute | solution.py:305
  58.9 1.8 %collective-permute-done.2 = f32[8,2048]{1,0:T(8,128)S(1)} collective-permute-done((f32[8,2048]{1,0:T(8,128)S(1)}, f32[8,2048]{1,0:T(8,128)S(1)}, u32[]{:S(2)}, u32[]{:S(2)}) %collective-permute-start.2) | collective-permute-done | bytes 65568 | tf_op jit(solution)/shard_map/ppermute | solution.py:305
  60.7 2.4 %collective-permute-done.3 = f32[8,2048]{1,0:T(8,128)S(1)} collective-permute-done((f32[8,2048]{1,0:T(8,128)S(1)}, f32[8,2048]{1,0:T(8,128)S(1)}, u32[]{:S(2)}, u32[]{:S(2)}) %collective-permute-start.3) | collective-permute-done | bytes 65568 | tf_op jit(solution)/shard_map/ppermute | solution.py:305
  63.0 1.5 %collective-permute-start.4 = (f32[8,2048]{1,0:T(8,128)S(1)}, f32[8,2048]{1,0:T(8,128)S(1)}, u32[]{:S(2)}, u32[]{:S(2)}) collective-permute-start(f32[8,2048]{1,0:T(8,128)S(1)} %add_add_fusion.1), channel_id=1, source_target_pairs={{0,2},{1,3},{2,0},{3,1},{4,6},{5,7},{6,4},{7,5},{8,10},{9,11},{10,... | collective-permute-start | bytes 196616 | tf_op jit(solution)/shard_map/ppermute | solution.py:305
  64.6 2.5 %collective-permute-start.5 = (f32[8,2048]{1,0:T(8,128)S(1)}, f32[8,2048]{1,0:T(8,128)S(1)}, u32[]{:S(2)}, u32[]{:S(2)}) collective-permute-start(f32[8,2048]{1,0:T(8,128)S(1)} %add_add_fusion.1), channel_id=1, source_target_pairs={{0,4},{1,5},{2,6},{3,7},{4,0},{5,1},{6,2},{7,3},{8,12},{9,13},{10,... | collective-permute-start | bytes 196616 | tf_op jit(solution)/shard_map/ppermute | solution.py:305
  67.5 3.6 %collective-permute-done.5 = f32[8,2048]{1,0:T(8,128)S(1)} collective-permute-done((f32[8,2048]{1,0:T(8,128)S(1)}, f32[8,2048]{1,0:T(8,128)S(1)}, u32[]{:S(2)}, u32[]{:S(2)}) %collective-permute-start.5) | collective-permute-done | bytes 65568 | tf_op jit(solution)/shard_map/ppermute | solution.py:305
  71.2 2.0 %collective-permute-done.6 = f32[8,2048]{1,0:T(8,128)S(1)} collective-permute-done((f32[8,2048]{1,0:T(8,128)S(1)}, f32[8,2048]{1,0:T(8,128)S(1)}, u32[]{:S(2)}, u32[]{:S(2)}) %collective-permute-start.6) | collective-permute-done | bytes 65568 | tf_op jit(solution)/shard_map/ppermute | solution.py:305
  73.8 10.9 %adjoint.1 = (f32[32,16,128]{2,1,0:T(8,128)}, f32[1]{0:T(128)}, bf16[8,4,1024,256]{3,2,1,0:T(8,128)(2,1)S(1)}, bf16[8,4,1024,256]{3,2,1,0:T(8,128)(2,1)S(1)}) custom-call(s32[2,32]{1,0:T(2,128)} %copy-done.1, f32[4]{0:T(128)} %wave_ref.5, f32[8,2048]{1,0:T(8,128)} %add_add_fusion.far_ref, ...), custom_call_target="tpu_custom_call", output_to_operand_aliasing={{2}: (7, {}), {3}: (8, {})} | custom-call | tf_op jit(solution)/shard_map/adjoint/pallas_call | solution.py:392
  84.7 2.6 %all-to-all-start.2 = ((f32[32,16,128]{2,1,0:T(8,128)}), f32[32,16,128]{2,1,0:T(8,128)S(1)}, u32[]{:S(2)}, u32[]{:S(2)}) async-start(f32[32,16,128]{2,1,0:T(8,128)} %get-tuple-element.20), calls=%async_computation.2 | async-start | bytes 524288 | tf_op jit(solution)/shard_map/all_to_all | solution.py:408
  88.0 10.0 %all-to-all-done.2.value_ref = f32[32,16,128]{2,1,0:T(8,128)S(1)} async-done(((f32[32,16,128]{2,1,0:T(8,128)}), f32[32,16,128]{2,1,0:T(8,128)S(1)}, u32[]{:S(2)}, u32[]{:S(2)}) %all-to-all-start.2) | async-done | bytes 262176 | tf_op jit(solution)/shard_map/all_to_all | solution.py:408
  98.0 5.0 %scatter_rows.1 = f32[16,8192]{1,0:T(8,128)} custom-call(f32[32,16,128]{2,1,0:T(8,128)S(1)} %all-to-all-done.2.value_ref, s32[32,1,128]{2,1,0:T(1,128)S(1)} %bitcast.8), custom_call_target="tpu_custom_call" | custom-call | tf_op jit(solution)/shard_map/scatter_rows/pallas_call | solution.py:409
  (25 shorter events, 5.5 us)
Async XLA Ops:
  3.2 15.0 %all-to-all-start = ((f32[32,8,128]{2,1,0:T(8,128)}), f32[32,8,128]{2,1,0:T(8,128)S(1)}, u32[]{:S(2)}, u32[]{:S(2)}) async-start(f32[32,8,128]{2,1,0:T(8,128)} %bitcast.1.rows_ref), calls=%async_computation | async-start | bytes 262144 | tf_op jit(solution)/shard_map/all_to_all | solution.py:329
  11.4 1.1 %copy-start = (f32[16,8192]{1,0:T(8,128)S(1)}, f32[16,8192]{1,0:T(8,128)}, u32[]{:S(2)}) copy-start(f32[16,8192]{1,0:T(8,128)} %cell_ref.1) | copy-start | bytes 1572868
  18.3 6.6 %copy-start.4 = (f32[32,8,128]{2,1,0:T(8,128)}, f32[32,8,128]{2,1,0:T(8,128)S(1)}, u32[]{:S(2)}) copy-start(f32[32,8,128]{2,1,0:T(8,128)S(1)} %all-to-all-done.came_ref) | copy-start | bytes 393220
  18.3 18.5 %all-to-all-start.1 = ((f32[32,16,128]{2,1,0:T(8,128)}), f32[32,16,128]{2,1,0:T(8,128)S(1)}, u32[]{:S(2)}, u32[]{:S(2)}) async-start(f32[32,16,128]{2,1,0:T(8,128)} %gather_rows.1), calls=%async_computation.1 | async-start | bytes 524288 | tf_op jit(solution)/shard_map/all_to_all | solution.py:339
  24.9 0.7 copy-start.2
  25.5 11.3 %copy-start.1 = (s32[2,32]{1,0:T(2,128)}, s32[2,32]{1,0:T(2,128)S(1)}, u32[]{:S(2)}) copy-start(s32[2,32]{1,0:T(2,128)S(1)} %convert_element_type.7.ends_ref) | copy-start | bytes 772
  36.8 0.7 copy-start.3
  52.2 1.5 %collective-permute-start = (f32[8,2048]{1,0:T(8,128)}, f32[8,2048]{1,0:T(8,128)S(1)}, u32[]{:S(2)}, u32[]{:S(2)}) collective-permute-start(f32[8,2048]{1,0:T(8,128)} %get-tuple-element.16), channel_id=1, source_target_pairs={{0,8},{1,9},{2,10},{3,11},{4,12},{5,13},{6,14},{7,15},{8,0},{9,1},... | collective-permute-start | bytes 196616 | tf_op jit(solution)/shard_map/ppermute | solution.py:305
  54.6 4.3 %collective-permute-start.1 = (f32[8,2048]{1,0:T(8,128)S(1)}, f32[8,2048]{1,0:T(8,128)S(1)}, u32[]{:S(2)}, u32[]{:S(2)}) collective-permute-start(f32[8,2048]{1,0:T(8,128)S(1)} %add.24), channel_id=1, source_target_pairs={{0,1},{1,0},{2,3},{3,2},{4,5},{5,4},{6,7},{7,6},{8,9},{9,8},{10,11... | collective-permute-start | bytes 196616 | tf_op jit(solution)/shard_map/ppermute | solution.py:305
  56.4 4.3 %collective-permute-start.2 = (f32[8,2048]{1,0:T(8,128)S(1)}, f32[8,2048]{1,0:T(8,128)S(1)}, u32[]{:S(2)}, u32[]{:S(2)}) collective-permute-start(f32[8,2048]{1,0:T(8,128)S(1)} %add.24), channel_id=1, source_target_pairs={{0,16},{1,17},{2,18},{3,19},{4,20},{5,21},{6,22},{7,23},{8,24},{9,... | collective-permute-start | bytes 196616 | tf_op jit(solution)/shard_map/ppermute | solution.py:305
  57.9 5.2 %collective-permute-start.3 = (f32[8,2048]{1,0:T(8,128)S(1)}, f32[8,2048]{1,0:T(8,128)S(1)}, u32[]{:S(2)}, u32[]{:S(2)}) collective-permute-start(f32[8,2048]{1,0:T(8,128)S(1)} %add.24), channel_id=1, source_target_pairs={{0,17},{1,16},{2,19},{3,18},{4,21},{5,20},{6,23},{7,22},{8,25},{9,... | collective-permute-start | bytes 196616 | tf_op jit(solution)/shard_map/ppermute | solution.py:305
  63.0 4.5 %collective-permute-start.4 = (f32[8,2048]{1,0:T(8,128)S(1)}, f32[8,2048]{1,0:T(8,128)S(1)}, u32[]{:S(2)}, u32[]{:S(2)}) collective-permute-start(f32[8,2048]{1,0:T(8,128)S(1)} %add_add_fusion.1), channel_id=1, source_target_pairs={{0,2},{1,3},{2,0},{3,1},{4,6},{5,7},{6,4},{7,5},{8,10},{9,11},{10,... | collective-permute-start | bytes 196616 | tf_op jit(solution)/shard_map/ppermute | solution.py:305
  64.6 6.6 %collective-permute-start.5 = (f32[8,2048]{1,0:T(8,128)S(1)}, f32[8,2048]{1,0:T(8,128)S(1)}, u32[]{:S(2)}, u32[]{:S(2)}) collective-permute-start(f32[8,2048]{1,0:T(8,128)S(1)} %add_add_fusion.1), channel_id=1, source_target_pairs={{0,4},{1,5},{2,6},{3,7},{4,0},{5,1},{6,2},{7,3},{8,12},{9,13},{10,... | collective-permute-start | bytes 196616 | tf_op jit(solution)/shard_map/ppermute | solution.py:305
  67.0 6.1 %collective-permute-start.6 = (f32[8,2048]{1,0:T(8,128)S(1)}, f32[8,2048]{1,0:T(8,128)S(1)}, u32[]{:S(2)}, u32[]{:S(2)}) collective-permute-start(f32[8,2048]{1,0:T(8,128)S(1)} %add_add_fusion.1), channel_id=1, source_target_pairs={{0,6},{1,7},{2,4},{3,5},{4,2},{5,3},{6,0},{7,1},{8,14},{9,15},{10,... | collective-permute-start | bytes 196616 | tf_op jit(solution)/shard_map/ppermute | solution.py:305
  73.8 13.6 %copy-start.5 = (f32[8,2048]{1,0:T(8,128)S(1)}, f32[8,2048]{1,0:T(8,128)}, u32[]{:S(2)}) copy-start(f32[8,2048]{1,0:T(8,128)} %add_add_fusion.far_ref) | copy-start | bytes 196612
  84.7 13.3 %all-to-all-start.2 = ((f32[32,16,128]{2,1,0:T(8,128)}), f32[32,16,128]{2,1,0:T(8,128)S(1)}, u32[]{:S(2)}, u32[]{:S(2)}) async-start(f32[32,16,128]{2,1,0:T(8,128)} %get-tuple-element.20), calls=%async_computation.2 | async-start | bytes 524288 | tf_op jit(solution)/shard_map/all_to_all | solution.py:408

commit v3 on v2

--- a/solution.py
+++ b/solution.py
@@ -54,8 +54,7 @@
         a2_ref[h * 16 : (h + 1) * 16, :] = (part - top.astype(F32)).astype(BF16)
     tiles = out_ref.shape[0]
 
-    @pl.loop(0, tiles // chunk)
-    def _(step):
+    for step in range(tiles // chunk):
         width = chunk * LANES
         base = step * chunk
         cell = jnp.concatenate([index_ref[base + t] for t in range(chunk)], axis=1)
@@ -168,12 +167,7 @@
     basis1 = basis_ref[0:4, first]
     basis2 = basis_ref[0:4, second]
     far1, far2 = [], []
-    for copy in fetch(step):
-        copy.wait()
     for f in range(FREQS):
-        total_t = jnp.dot(src_ref[f, 0], t_ref[step, f], preferred_element_type=F32)
-        total_s = jnp.dot(src_ref[f, 1], s_ref[step, f], preferred_element_type=F32)
-        far1 += project(f, total_t, total_s, basis1)
         parts = masked_parts(parts_ref, f)
         for i in range(live_own // PIECE):
             at = slice(i * PIECE, (i + 1) * PIECE)
@@ -182,6 +176,12 @@
         total_t = jnp.dot(src_ref[f, 0], t_ref[steps + step, f], preferred_element_type=F32)
         total_s = jnp.dot(src_ref[f, 1], s_ref[steps + step, f], preferred_element_type=F32)
         far2 += project(f, total_t, total_s, basis2)
+    for copy in fetch(step):
+        copy.wait()
+    for f in range(FREQS):
+        total_t = jnp.dot(src_ref[f, 0], t_ref[step, f], preferred_element_type=F32)
+        total_s = jnp.dot(src_ref[f, 1], s_ref[step, f], preferred_element_type=F32)
+        far1 += project(f, total_t, total_s, basis1)
     far_ref[:, first] = jnp.concatenate(far1, axis=0)
     far_ref[:, second] = jnp.concatenate(far2, axis=0)
 
@@ -252,16 +252,15 @@
         lo = cell & 255
         level = lax.broadcasted_iota(jnp.int32, (256, width), 0)
         pick = jnp.where(level == lo, 1.0, 0.0).astype(BF16)
-        top = value.astype(BF16)
-        rest = (value - top.astype(F32)).astype(BF16)
+        value = value.astype(BF16)
         hi = jnp.broadcast_to(hi, (16, width)).astype(F32).astype(BF16)
         zero = jnp.zeros((16, width), BF16)
-        tops = jnp.concatenate([jnp.where(hi == float(h), top, zero) for h in range(high)], axis=0)
-        rests = jnp.concatenate([jnp.where(hi == float(h), rest, zero) for h in range(high)], axis=0)
-        total = total + lax.dot_general(tops, pick, contract, preferred_element_type=F32)
-        return total + lax.dot_general(rests, pick, contract, preferred_element_type=F32)
-
-    total = lax.fori_loop(0, tiles // chunk, body, jnp.zeros((high * 16, 256), F32))
+        spread = jnp.concatenate([jnp.where(hi == float(h), value, zero) for h in range(high)], axis=0)
+        return total + lax.dot_general(spread, pick, contract, preferred_element_type=F32)
+
+    total = jnp.zeros((high * 16, 256), F32)
+    for step in range(tiles // chunk):
+        total = body(step, total)
     for h in range(high):
         out_ref[:, h * 256 : (h + 1) * 256] = total[h * 16 : (h + 1) * 16, :]
 
@@ -349,12 +348,11 @@
     packs = live_own // LANES + 1
     first = pltpu.HBM((half, FREQS, live_own, width), BF16)
     held = pltpu.VMEM((2 * half, FREQS, live_own, width), BF16)
-    by_dir = lambda i: (0, i)
     block = pl.BlockSpec((1, FREQS, live_own, width), lambda i: (i, 0, 0, 0))
     first_t, first_s, kept, turned = pl.pallas_call(
         phase_kernel,
         grid=(half,),
-        in_specs=[smem(), smem(), vmem, pl.BlockSpec((32 * FREQS, width), by_dir)],
+        in_specs=[smem(), smem(), vmem, pl.BlockSpec((32 * FREQS, width), lambda i: (0, i))],
         out_specs=[block, block, vmem, vmem],
         out_shape=[
             first, first,

time: 104 us -> 99 us (0.952)
  Pallas kernels: 47.2 us -> 42.6 us
  waiting for transfers between devices: 22.1 us -> 23.4 us
  starting transfers between devices: 23.6 us -> 22.4 us
    pallas_call x1, Pallas kernels: 4.97 us -> 2.08 us  [on_device(): pl.pallas_call(functools.partial(scatter_kernel, chunk=4), in_specs=[vmem...]
    pallas_call x1, Pallas kernels: 5.38 us -> 4.11 us  [on_device(): pl.pallas_call(functools.partial(gather_kernel, chunk=4), in_specs=[vmem,...]
    all_to_all x1, waiting for transfers between devices: 0.44 us -> 1.7 us  [on_device(): came = lax.all_to_all(rows, AXES, split_axis=0, concat_axis=0, tiled=True)]
    all_to_all x1, starting transfers between devices: 5.39 us -> 4.31 us  [on_device(): lax.all_to_all(from_tiles(outgoing, cap), AXES, split_axis=0, concat_axis...]
where the time goes in v3:
time: 99 us; the launch traced here: 98.3 us
  Pallas kernels  42.6 us (43%)
  waiting for transfers between devices  23.4 us (24%)
  starting transfers between devices  22.4 us (23%)
  local copies, waits for them, and re-layouts  6.19 us (6%)
  other arithmetic  2.36 us (2%)
  between operations  1.4 us (1%)
    pallas_call x1, Pallas kernels, on_device(): pl.pallas_call(radiate_kernel, grid=(half,), in_specs=[smem(), smem(), vm...  14.2 us
    ppermute x7, waiting for transfers between devices, all_sum(): lax.ppermute(x, AXES, [(i, i ^ m) for i in range(gx * gy)])  11.7 us
    pallas_call x1, Pallas kernels, on_device(): pl.pallas_call(phase_kernel, grid=(half,), in_specs=[smem(), smem(), vmem...  11.3 us
    pallas_call x1, Pallas kernels, on_device(): pl.pallas_call(adjoint_kernel, in_specs=[smem(), smem()] + [vmem] * 7, ou...  10.9 us
    all_to_all x1, waiting for transfers between devices, on_device(): lax.all_to_all(back[:, :, :cap], AXES, split_axis=0, concat_axis=0, tiled...  9.96 us
    ppermute x7, starting transfers between devices, all_sum(): lax.ppermute(x, AXES, [(i, i ^ m) for i in range(gx * gy)])  8.14 us
    all_to_all x1, starting transfers between devices, on_device(): came = lax.all_to_all(rows, AXES, split_axis=0, concat_axis=0, tiled=True)  7.3 us
    all_to_all x1, starting transfers between devices, on_device(): lax.all_to_all(from_tiles(outgoing, cap), AXES, split_axis=0, concat_axis...  4.31 us
  transfers between devices with their start and end apart: 10, of which 8 were waited for; matrix products, arithmetic and copies ran while one was open for 3% of the time, Pallas kernels for 16%

profile of v3, /device:TPU:0, one launch (start us, length us, event | category | flops | bytes accessed | tf_op | source)
XLA Modules:
  0.0 98.3 jit_solution(14451426967158633555)
XLA Ops:
  1.3 0.9 concatenate.3
  2.4 0.8 copy.17
  3.2 7.3 %all-to-all-start = ((f32[32,8,128]{2,1,0:T(8,128)}), f32[32,8,128]{2,1,0:T(8,128)S(1)}, u32[]{:S(2)}, u32[]{:S(2)}) async-start(f32[32,8,128]{2,1,0:T(8,128)} %bitcast.1.rows_ref), calls=%async_computation | async-start | bytes 262144 | tf_op jit(solution)/shard_map/all_to_all | solution.py:328
  11.4 1.1 %copy-done = f32[16,8192]{1,0:T(8,128)S(1)} copy-done((f32[16,8192]{1,0:T(8,128)S(1)}, f32[16,8192]{1,0:T(8,128)}, u32[]{:S(2)}) %copy-start) | copy-done | bytes 524312
  12.4 4.1 %gather_rows.1 = f32[32,16,128]{2,1,0:T(8,128)} custom-call(f32[16,8192]{1,0:T(8,128)S(1)} %copy-done, s32[32,1,128]{2,1,0:T(1,128)S(1)} %bitcast.7, f32[32,8,128]{2,1,0:T(8,128)} %bitcast.1.rows_ref), custom_call_target="tpu_custom_call" | custom-call | tf_op jit(solution)/shard_map/gather_rows/pallas_call | solution.py:330
  16.6 1.7 %all-to-all-done.came_ref = f32[32,8,128]{2,1,0:T(8,128)S(1)} async-done(((f32[32,8,128]{2,1,0:T(8,128)}), f32[32,8,128]{2,1,0:T(8,128)S(1)}, u32[]{:S(2)}, u32[]{:S(2)}) %all-to-all-start) | async-done | bytes 131104 | tf_op jit(solution)/shard_map/all_to_all | solution.py:328
  18.3 4.3 %all-to-all-start.1 = ((f32[32,16,128]{2,1,0:T(8,128)}), f32[32,16,128]{2,1,0:T(8,128)S(1)}, u32[]{:S(2)}, u32[]{:S(2)}) async-start(f32[32,16,128]{2,1,0:T(8,128)} %gather_rows.1), calls=%async_computation.1 | async-start | bytes 524288 | tf_op jit(solution)/shard_map/all_to_all | solution.py:338
  22.9 0.8 multiply_reduce_fusion
  24.4 11.3 %phases.1 = (bf16[4,4,1024,256]{3,2,1,0:T(8,128)(2,1)}, bf16[4,4,1024,256]{3,2,1,0:T(8,128)(2,1)}, f32[8,1024]{1,0:T(8,128)}, bf16[1024,128]{1,0:T(8,128)(2,1)}) custom-call(s32[2,32]{1,0:T(2,128)S(1)} %convert_element_type.7.ends_ref, f32[4]{0:T(128)S(1)} %copy-done.2, f32[32,8,128]{2,1,0:T(8,128)} %copy-done.4, bf16[128,2048]{1,0:T(8,128)(2,1)} %constant.31.clone.parts_ref), custom_call_target="tpu_custom_call" | custom-call | tf_op jit(solution)/shard_map/phases/pallas_call | solution.py:352
  36.4 14.2 %radiate.1 = (f32[8,2048]{1,0:T(8,128)}, bf16[8,4,1024,256]{3,2,1,0:T(8,128)(2,1)S(1)}, bf16[8,4,1024,256]{3,2,1,0:T(8,128)(2,1)S(1)}) custom-call(s32[2,32]{1,0:T(2,128)} %copy-done.1, f32[4]{0:T(128)} %wave_ref.5, f32[32,16,128]{2,1,0:T(8,128)} %copy-done.3, f32[8,1024]{1,0:T(8,128)} %get-tuple-element.12.rows_ref, ...), custom_call_target="tpu_custom_call" | custom-call | tf_op jit(solution)/shard_map/radiate/pallas_call | solution.py:368
  50.8 1.4 %collective-permute-done = f32[8,2048]{1,0:T(8,128)S(1)} collective-permute-done((f32[8,2048]{1,0:T(8,128)}, f32[8,2048]{1,0:T(8,128)S(1)}, u32[]{:S(2)}, u32[]{:S(2)}) %collective-permute-start) | collective-permute-done | bytes 65568 | tf_op jit(solution)/shard_map/ppermute | solution.py:304
  52.2 0.9 add.24
  53.0 1.7 %collective-permute-start.1 = (f32[8,2048]{1,0:T(8,128)S(1)}, f32[8,2048]{1,0:T(8,128)S(1)}, u32[]{:S(2)}, u32[]{:S(2)}) collective-permute-start(f32[8,2048]{1,0:T(8,128)S(1)} %add.24), channel_id=1, source_target_pairs={{0,1},{1,0},{2,3},{3,2},{4,5},{5,4},{6,7},{7,6},{8,9},{9,8},{10,11... | collective-permute-start | bytes 196616 | tf_op jit(solution)/shard_map/ppermute | solution.py:304
  54.7 1.5 %collective-permute-start.2 = (f32[8,2048]{1,0:T(8,128)S(1)}, f32[8,2048]{1,0:T(8,128)S(1)}, u32[]{:S(2)}, u32[]{:S(2)}) collective-permute-start(f32[8,2048]{1,0:T(8,128)S(1)} %add.24), channel_id=1, source_target_pairs={{0,16},{1,17},{2,18},{3,19},{4,20},{5,21},{6,22},{7,23},{8,24},{9,... | collective-permute-start | bytes 196616 | tf_op jit(solution)/shard_map/ppermute | solution.py:304
  57.4 1.6 %collective-permute-done.2 = f32[8,2048]{1,0:T(8,128)S(1)} collective-permute-done((f32[8,2048]{1,0:T(8,128)S(1)}, f32[8,2048]{1,0:T(8,128)S(1)}, u32[]{:S(2)}, u32[]{:S(2)}) %collective-permute-start.2) | collective-permute-done | bytes 65568 | tf_op jit(solution)/shard_map/ppermute | solution.py:304
  59.0 2.4 %collective-permute-done.3 = f32[8,2048]{1,0:T(8,128)S(1)} collective-permute-done((f32[8,2048]{1,0:T(8,128)S(1)}, f32[8,2048]{1,0:T(8,128)S(1)}, u32[]{:S(2)}, u32[]{:S(2)}) %collective-permute-start.3) | collective-permute-done | bytes 65568 | tf_op jit(solution)/shard_map/ppermute | solution.py:304
  61.4 1.5 %collective-permute-start.4 = (f32[8,2048]{1,0:T(8,128)S(1)}, f32[8,2048]{1,0:T(8,128)S(1)}, u32[]{:S(2)}, u32[]{:S(2)}) collective-permute-start(f32[8,2048]{1,0:T(8,128)S(1)} %add_add_fusion.1), channel_id=1, source_target_pairs={{0,2},{1,3},{2,0},{3,1},{4,6},{5,7},{6,4},{7,5},{8,10},{9,11},{10,... | collective-permute-start | bytes 196616 | tf_op jit(solution)/shard_map/ppermute | solution.py:304
  62.9 2.5 %collective-permute-start.5 = (f32[8,2048]{1,0:T(8,128)S(1)}, f32[8,2048]{1,0:T(8,128)S(1)}, u32[]{:S(2)}, u32[]{:S(2)}) collective-permute-start(f32[8,2048]{1,0:T(8,128)S(1)} %add_add_fusion.1), channel_id=1, source_target_pairs={{0,4},{1,5},{2,6},{3,7},{4,0},{5,1},{6,2},{7,3},{8,12},{9,13},{10,... | collective-permute-start | bytes 196616 | tf_op jit(solution)/shard_map/ppermute | solution.py:304
  65.8 3.6 %collective-permute-done.5 = f32[8,2048]{1,0:T(8,128)S(1)} collective-permute-done((f32[8,2048]{1,0:T(8,128)S(1)}, f32[8,2048]{1,0:T(8,128)S(1)}, u32[]{:S(2)}, u32[]{:S(2)}) %collective-permute-start.5) | collective-permute-done | bytes 65568 | tf_op jit(solution)/shard_map/ppermute | solution.py:304
  69.5 2.0 %collective-permute-done.6 = f32[8,2048]{1,0:T(8,128)S(1)} collective-permute-done((f32[8,2048]{1,0:T(8,128)S(1)}, f32[8,2048]{1,0:T(8,128)S(1)}, u32[]{:S(2)}, u32[]{:S(2)}) %collective-permute-start.6) | collective-permute-done | bytes 65568 | tf_op jit(solution)/shard_map/ppermute | solution.py:304
  72.1 10.9 %adjoint.1 = (f32[32,16,128]{2,1,0:T(8,128)}, f32[1]{0:T(128)}, bf16[8,4,1024,256]{3,2,1,0:T(8,128)(2,1)S(1)}, bf16[8,4,1024,256]{3,2,1,0:T(8,128)(2,1)S(1)}) custom-call(s32[2,32]{1,0:T(2,128)} %copy-done.1, f32[4]{0:T(128)} %wave_ref.5, f32[8,2048]{1,0:T(8,128)} %add_add_fusion.far_ref, ...), custom_call_target="tpu_custom_call", output_to_operand_aliasing={{2}: (7, {}), {3}: (8, {})} | custom-call | tf_op jit(solution)/shard_map/adjoint/pallas_call | solution.py:390
  83.0 2.6 %all-to-all-start.2 = ((f32[32,16,128]{2,1,0:T(8,128)}), f32[32,16,128]{2,1,0:T(8,128)S(1)}, u32[]{:S(2)}, u32[]{:S(2)}) async-start(f32[32,16,128]{2,1,0:T(8,128)} %get-tuple-element.20), calls=%async_computation.2 | async-start | bytes 524288 | tf_op jit(solution)/shard_map/all_to_all | solution.py:406
  86.3 10.0 %all-to-all-done.2.value_ref = f32[32,16,128]{2,1,0:T(8,128)S(1)} async-done(((f32[32,16,128]{2,1,0:T(8,128)}), f32[32,16,128]{2,1,0:T(8,128)S(1)}, u32[]{:S(2)}, u32[]{:S(2)}) %all-to-all-start.2) | async-done | bytes 262176 | tf_op jit(solution)/shard_map/all_to_all | solution.py:406
  96.3 2.1 %scatter_rows.1 = f32[16,8192]{1,0:T(8,128)} custom-call(f32[32,16,128]{2,1,0:T(8,128)S(1)} %all-to-all-done.2.value_ref, s32[32,1,128]{2,1,0:T(1,128)S(1)} %bitcast.8), custom_call_target="tpu_custom_call" | custom-call | tf_op jit(solution)/shard_map/scatter_rows/pallas_call | solution.py:407
  (25 shorter events, 5.8 us)
Async XLA Ops:
  3.2 15.0 %all-to-all-start = ((f32[32,8,128]{2,1,0:T(8,128)}), f32[32,8,128]{2,1,0:T(8,128)S(1)}, u32[]{:S(2)}, u32[]{:S(2)}) async-start(f32[32,8,128]{2,1,0:T(8,128)} %bitcast.1.rows_ref), calls=%async_computation | async-start | bytes 262144 | tf_op jit(solution)/shard_map/all_to_all | solution.py:328
  11.4 1.1 %copy-start = (f32[16,8192]{1,0:T(8,128)S(1)}, f32[16,8192]{1,0:T(8,128)}, u32[]{:S(2)}) copy-start(f32[16,8192]{1,0:T(8,128)} %cell_ref.1) | copy-start | bytes 1572868
  18.3 5.5 %copy-start.4 = (f32[32,8,128]{2,1,0:T(8,128)}, f32[32,8,128]{2,1,0:T(8,128)S(1)}, u32[]{:S(2)}) copy-start(f32[32,8,128]{2,1,0:T(8,128)S(1)} %all-to-all-done.came_ref) | copy-start | bytes 393220
  18.3 17.5 %all-to-all-start.1 = ((f32[32,16,128]{2,1,0:T(8,128)}), f32[32,16,128]{2,1,0:T(8,128)S(1)}, u32[]{:S(2)}, u32[]{:S(2)}) async-start(f32[32,16,128]{2,1,0:T(8,128)} %gather_rows.1), calls=%async_computation.1 | async-start | bytes 524288 | tf_op jit(solution)/shard_map/all_to_all | solution.py:338
  23.8 0.7 copy-start.2
  24.4 11.3 %copy-start.1 = (s32[2,32]{1,0:T(2,128)}, s32[2,32]{1,0:T(2,128)S(1)}, u32[]{:S(2)}) copy-start(s32[2,32]{1,0:T(2,128)S(1)} %convert_element_type.7.ends_ref) | copy-start | bytes 772
  35.7 0.7 copy-start.3
  50.7 1.5 %collective-permute-start = (f32[8,2048]{1,0:T(8,128)}, f32[8,2048]{1,0:T(8,128)S(1)}, u32[]{:S(2)}, u32[]{:S(2)}) collective-permute-start(f32[8,2048]{1,0:T(8,128)} %get-tuple-element.16), channel_id=1, source_target_pairs={{0,8},{1,9},{2,10},{3,11},{4,12},{5,13},{6,14},{7,15},{8,0},{9,1},... | collective-permute-start | bytes 196616 | tf_op jit(solution)/shard_map/ppermute | solution.py:304
  53.0 4.3 %collective-permute-start.1 = (f32[8,2048]{1,0:T(8,128)S(1)}, f32[8,2048]{1,0:T(8,128)S(1)}, u32[]{:S(2)}, u32[]{:S(2)}) collective-permute-start(f32[8,2048]{1,0:T(8,128)S(1)} %add.24), channel_id=1, source_target_pairs={{0,1},{1,0},{2,3},{3,2},{4,5},{5,4},{6,7},{7,6},{8,9},{9,8},{10,11... | collective-permute-start | bytes 196616 | tf_op jit(solution)/shard_map/ppermute | solution.py:304
  54.7 4.3 %collective-permute-start.2 = (f32[8,2048]{1,0:T(8,128)S(1)}, f32[8,2048]{1,0:T(8,128)S(1)}, u32[]{:S(2)}, u32[]{:S(2)}) collective-permute-start(f32[8,2048]{1,0:T(8,128)S(1)} %add.24), channel_id=1, source_target_pairs={{0,16},{1,17},{2,18},{3,19},{4,20},{5,21},{6,22},{7,23},{8,24},{9,... | collective-permute-start | bytes 196616 | tf_op jit(solution)/shard_map/ppermute | solution.py:304
  56.2 5.2 %collective-permute-start.3 = (f32[8,2048]{1,0:T(8,128)S(1)}, f32[8,2048]{1,0:T(8,128)S(1)}, u32[]{:S(2)}, u32[]{:S(2)}) collective-permute-start(f32[8,2048]{1,0:T(8,128)S(1)} %add.24), channel_id=1, source_target_pairs={{0,17},{1,16},{2,19},{3,18},{4,21},{5,20},{6,23},{7,22},{8,25},{9,... | collective-permute-start | bytes 196616 | tf_op jit(solution)/shard_map/ppermute | solution.py:304
  61.4 4.5 %collective-permute-start.4 = (f32[8,2048]{1,0:T(8,128)S(1)}, f32[8,2048]{1,0:T(8,128)S(1)}, u32[]{:S(2)}, u32[]{:S(2)}) collective-permute-start(f32[8,2048]{1,0:T(8,128)S(1)} %add_add_fusion.1), channel_id=1, source_target_pairs={{0,2},{1,3},{2,0},{3,1},{4,6},{5,7},{6,4},{7,5},{8,10},{9,11},{10,... | collective-permute-start | bytes 196616 | tf_op jit(solution)/shard_map/ppermute | solution.py:304
  62.9 6.6 %collective-permute-start.5 = (f32[8,2048]{1,0:T(8,128)S(1)}, f32[8,2048]{1,0:T(8,128)S(1)}, u32[]{:S(2)}, u32[]{:S(2)}) collective-permute-start(f32[8,2048]{1,0:T(8,128)S(1)} %add_add_fusion.1), channel_id=1, source_target_pairs={{0,4},{1,5},{2,6},{3,7},{4,0},{5,1},{6,2},{7,3},{8,12},{9,13},{10,... | collective-permute-start | bytes 196616 | tf_op jit(solution)/shard_map/ppermute | solution.py:304
  65.3 6.1 %collective-permute-start.6 = (f32[8,2048]{1,0:T(8,128)S(1)}, f32[8,2048]{1,0:T(8,128)S(1)}, u32[]{:S(2)}, u32[]{:S(2)}) collective-permute-start(f32[8,2048]{1,0:T(8,128)S(1)} %add_add_fusion.1), channel_id=1, source_target_pairs={{0,6},{1,7},{2,4},{3,5},{4,2},{5,3},{6,0},{7,1},{8,14},{9,15},{10,... | collective-permute-start | bytes 196616 | tf_op jit(solution)/shard_map/ppermute | solution.py:304
  72.1 13.6 %copy-start.5 = (f32[8,2048]{1,0:T(8,128)S(1)}, f32[8,2048]{1,0:T(8,128)}, u32[]{:S(2)}) copy-start(f32[8,2048]{1,0:T(8,128)} %add_add_fusion.far_ref) | copy-start | bytes 196612
  83.0 13.3 %all-to-all-start.2 = ((f32[32,16,128]{2,1,0:T(8,128)}), f32[32,16,128]{2,1,0:T(8,128)S(1)}, u32[]{:S(2)}, u32[]{:S(2)}) async-start(f32[32,16,128]{2,1,0:T(8,128)} %get-tuple-element.20), calls=%async_computation.2 | async-start | bytes 524288 | tf_op jit(solution)/shard_map/all_to_all | solution.py:406

commit v4 on v3

--- a/solution.py
+++ b/solution.py
@@ -129,7 +129,7 @@
 
 def radiate_kernel(
     ends_ref, wave_ref, came_ref, rows_ref, y_ref, parts_ref, basis_ref, first_t_ref, first_s_ref,
-    far_ref, t_ref, s_ref, packed_ref, src_ref, t_sem, s_sem,
+    t_ref, s_ref, far_ref, packed_ref, src_ref, t_sem, s_sem,
 ):
     live_own = rows_ref.shape[1]
     step = pl.program_id(0)
@@ -187,14 +187,22 @@
 
 
 def adjoint_kernel(
-    ends_ref, wave_ref, far_ref, target_ref, weight_ref, basis_ref, rows_ref,
-    t_ref, s_ref, out_ref, cost_ref, _t, _s, flat_ref,
+    ends_ref, wave_ref, target_ref, weight_ref, basis_ref, rows_ref, t_ref, s_ref, *rest
 ):
+    far_terms, (_t, _s, out_ref, cost_ref, far_ref, flat_ref) = rest[:-6], rest[-6:]
+    far = far_terms[0][...]
+    if len(far_terms) == 2:
+        far = far + far_terms[1][...]
+    else:
+        far = (far + far_terms[1][...]) + (far_terms[2][...] + far_terms[3][...])
+    for f in range(FREQS):
+        far_ref[f] = far[2 * f : 2 * f + 2]
+
     live_own = rows_ref.shape[1]
     blocks = live_own // LANES
-    count_dirs = far_ref.shape[1]
+    count_dirs = far.shape[1]
     width = t_ref.shape[3]
-    mismatch = far_ref[...] - jnp.concatenate([target_ref[f] for f in range(FREQS)], axis=0)
+    mismatch = far - jnp.concatenate([target_ref[f] for f in range(FREQS)], axis=0)
     pull = weight_ref[...] * mismatch
     cost_ref[0] = jnp.sum(pull * mismatch) / count_dirs
     gradient = pull * (2.0 / count_dirs)
@@ -302,11 +310,9 @@
     for bits in rounds:
         masks = [sum(1 << b for k, b in enumerate(bits) if code >> k & 1) for code in range(1, 1 << len(bits))]
         came = [lax.ppermute(x, AXES, [(i, i ^ m) for i in range(gx * gy)]) for m in masks]
-        if len(came) == 1:
-            x = x + came[0]
-        else:
-            x = (x + came[0]) + (came[1] + came[2])
-    return x
+        if bits is rounds[-1]:
+            return [x] + came
+        x = x + came[0] if len(came) == 1 else (x + came[0]) + (came[1] + came[2])
 
 
 def on_device(cell_state, geometry, surface_cell, counts, wavenumbers, target, direction_weight):
@@ -319,7 +325,10 @@
     tiles = rows_dev // LANES
     high = cells // 256
     basis, parts = direction_tables(count_dirs)
-    basis, parts = jnp.asarray(basis), jnp.asarray(parts)
+    basis, parts, wavenumbers, cell_state = (
+        pltpu.with_memory_space_constraint(x, pltpu.HBM)
+        for x in (jnp.asarray(basis), jnp.asarray(parts), wavenumbers, cell_state)
+    )
     vmem = pl.BlockSpec(memory_space=pltpu.VMEM)
 
     share = (counts // owners).astype(F32)
@@ -336,13 +345,13 @@
         name="gather_rows",
     )(cell_state, index, to_tiles(rows, cap))
     values = lax.all_to_all(from_tiles(outgoing, cap), AXES, split_axis=0, concat_axis=0, tiled=True)
-    marks = np.stack([np.tril(np.ones((owners, owners), np.float32), -1), np.eye(owners, dtype=np.float32)])
-    ends = jnp.sum(came[:, 7, 0] * marks, axis=2).astype(jnp.int32)
+    me, other = jnp.arange(2 * owners)[:, None], jnp.arange(owners)[None, :]
+    counted = jnp.where(me < owners, other < me, other == me - owners)
+    ends = jnp.sum(jnp.where(counted, came[:, 7, 0][None, :], 0.0), axis=1).astype(jnp.int32).reshape(2, owners)
     if cap < LANES:
         came = jnp.pad(came, ((0, 0), (0, 0), (0, LANES - cap)))
         values = jnp.pad(values, ((0, 0), (0, 0), (0, LANES - cap)))
 
-    parts, basis, came, values = (pltpu.with_memory_space_constraint(x, pltpu.HBM) for x in (parts, basis, came, values))
     width = 256
     half = count_dirs // width // 2
     packs = live_own // LANES + 1
@@ -365,7 +374,7 @@
     )(ends, wavenumbers, came, parts)
 
     hbm = pl.BlockSpec(memory_space=pltpu.HBM)
-    far, t_all, s_all = pl.pallas_call(
+    t_all, s_all, far = pl.pallas_call(
         radiate_kernel,
         grid=(half,),
         in_specs=[
@@ -374,7 +383,7 @@
             vmem, hbm, hbm,
         ],
         out_specs=[vmem] * 3,
-        out_shape=[jax.ShapeDtypeStruct((2 * FREQS, count_dirs), F32), held, held],
+        out_shape=[held, held, pltpu.VMEM((2 * FREQS, count_dirs), F32)],
         scratch_shapes=[
             pltpu.VMEM((packs, 16, LANES), F32),
             pltpu.VMEM((FREQS, 2, 8, live_own), BF16),
@@ -385,24 +394,25 @@
         name="radiate",
     )(ends, wavenumbers, values, kept, turned, parts, basis, first_t, first_s)
 
-    far = all_sum(far)
-
-    back, objective = pl.pallas_call(
+    far_terms = [pltpu.with_memory_space_constraint(x, pltpu.VMEM) for x in all_sum(far)]
+
+    _, _, back, objective, far = pl.pallas_call(
         adjoint_kernel,
-        in_specs=[smem(), smem()] + [vmem] * 7,
-        out_specs=[vmem, smem(), vmem, vmem],
+        in_specs=[smem(), smem()] + [vmem] * (6 + len(far_terms)),
+        out_specs=[vmem, vmem, vmem, smem(), vmem],
         out_shape=[
+            held, held,
             jax.ShapeDtypeStruct((owners, 16, LANES), F32),
             jax.ShapeDtypeStruct((1,), F32),
-            held, held,
+            jax.ShapeDtypeStruct(target.shape, F32),
         ],
-        input_output_aliases={7: 2, 8: 3},
+        input_output_aliases={6: 0, 7: 1},
         scratch_shapes=[pltpu.VMEM((packs, 16, LANES), F32)],
         compiler_params=params(),
         name="adjoint",
     )(
-        ends, wavenumbers, far, target, direction_weight.reshape(1, count_dirs), basis, kept, t_all, s_all,
-    )[:2]
+        ends, wavenumbers, target, direction_weight.reshape(1, count_dirs), basis, kept, t_all, s_all, *far_terms,
+    )
     returned = lax.all_to_all(back[:, :, :cap], AXES, split_axis=0, concat_axis=0, tiled=True)
     cell_adjoint = pl.pallas_call(
         functools.partial(scatter_kernel, chunk=4),
@@ -411,7 +421,7 @@
         compiler_params=params(),
         name="scatter_rows",
     )(to_tiles(returned, cap), index)
-    return (far.reshape(FREQS, 2, count_dirs), objective[0], cell_adjoint)
+    return (far, objective[0], cell_adjoint)
 
 
 def solution(mesh):

time: 99 us -> 93.1 us (0.940)
  blocking collectives: 0 us -> 14.6 us
  waiting for transfers between devices: 23.4 us -> 11.7 us
  starting transfers between devices: 22.4 us -> 18.9 us
  local copies, waits for them, and re-layouts: 6.19 us -> 3.88 us
  other arithmetic: 2.36 us -> 0.13 us
    all_to_all x0 -> x1, blocking collectives: none -> 14.6 us  [on_device(): lax.all_to_all(back[:, :, :cap], AXES, split_axis=0, concat_axis=0, tiled...]
    all_to_all x1 -> x0, waiting for transfers between devices: 9.96 us -> none  [on_device(): lax.all_to_all(back[:, :, :cap], AXES, split_axis=0, concat_axis=0, tiled...]
    all_to_all x1 -> x0, starting transfers between devices: 2.6 us -> none  [on_device(): lax.all_to_all(back[:, :, :cap], AXES, split_axis=0, concat_axis=0, tiled...]
    ppermute x7, waiting for transfers between devices: 11.7 us -> 9.13 us  [all_sum(): lax.ppermute(x, AXES, [(i, i ^ m) for i in range(gx * gy)])]
    unnamed x12 -> x4, local copies, waits for them, and re-layouts: 2.42 us -> 0.7 us
    add x3 -> x2, other arithmetic: 1.51 us -> 0.03 us  [all_sum(): x = x + came[0] if len(came) == 1 else x + came[0] + (came[1] + came[2])]
  transfers between devices with their start and end apart: 10 -> 9, of which waited for: 8 -> 7; matrix products, arithmetic and copies ran while one was open for 3% -> 1% of each run, Pallas kernels for 16% -> 17%
where the time goes in v4:
time: 93.1 us; the launch traced here: 92.6 us
  Pallas kernels  42.1 us (45%)
  starting transfers between devices  18.9 us (20%)
  blocking collectives  14.6 us (16%)
  waiting for transfers between devices  11.7 us (13%)
  local copies, waits for them, and re-layouts  3.88 us (4%)
  between operations  1.38 us (1%)
    all_to_all x1, blocking collectives, on_device(): lax.all_to_all(back[:, :, :cap], AXES, split_axis=0, concat_axis=0, tiled...  14.6 us
    pallas_call x1, Pallas kernels, on_device(): pl.pallas_call(radiate_kernel, grid=(half,), in_specs=[smem(), smem(), vm...  13.6 us
    pallas_call x1, Pallas kernels, on_device(): pl.pallas_call(phase_kernel, grid=(half,), in_specs=[smem(), smem(), vmem...  11.1 us
    pallas_call x1, Pallas kernels, on_device(): pl.pallas_call(adjoint_kernel, in_specs=[smem(), smem()] + [vmem] * (6 +...  10.9 us
    ppermute x7, waiting for transfers between devices, all_sum(): lax.ppermute(x, AXES, [(i, i ^ m) for i in range(gx * gy)])  9.13 us
    ppermute x7, starting transfers between devices, all_sum(): lax.ppermute(x, AXES, [(i, i ^ m) for i in range(gx * gy)])  8.12 us
    all_to_all x1, starting transfers between devices, on_device(): came = lax.all_to_all(rows, AXES, split_axis=0, concat_axis=0, tiled=True)  7.3 us
    pallas_call x1, Pallas kernels, on_device(): pl.pallas_call(functools.partial(gather_kernel, chunk=4), in_specs=[vmem,...  4.31 us
  transfers between devices with their start and end apart: 9, of which 7 were waited for; matrix products, arithmetic and copies ran while one was open for 1% of the time, Pallas kernels for 17%

profile of v4, /device:TPU:0, one launch (start us, length us, event | category | flops | bytes accessed | tf_op | source)
XLA Modules:
  0.0 92.6 jit_solution(10793921365843649957)
XLA Ops:
  1.3 0.9 concatenate.3
  2.4 0.8 copy.16
  3.2 7.3 %all-to-all-start = ((f32[32,8,128]{2,1,0:T(8,128)}), f32[32,8,128]{2,1,0:T(8,128)S(1)}, u32[]{:S(2)}, u32[]{:S(2)}) async-start(f32[32,8,128]{2,1,0:T(8,128)} %bitcast.1.rows_ref), calls=%async_computation | async-start | bytes 262144 | tf_op jit(solution)/shard_map/all_to_all | solution.py:337
  10.5 0.8 reshape.41
  11.4 4.3 %gather_rows.1 = f32[32,16,128]{2,1,0:T(8,128)} custom-call(f32[16,8192]{1,0:T(8,128)} %cell_ref.1, s32[32,1,128]{2,1,0:T(1,128)S(1)} %bitcast.7, f32[32,8,128]{2,1,0:T(8,128)} %bitcast.1.rows_ref), custom_call_target="tpu_custom_call" | custom-call | tf_op jit(solution)/shard_map/gather_rows/pallas_call | solution.py:339
  15.7 2.6 %all-to-all-done.came_ref = f32[32,8,128]{2,1,0:T(8,128)S(1)} async-done(((f32[32,8,128]{2,1,0:T(8,128)}), f32[32,8,128]{2,1,0:T(8,128)S(1)}, u32[]{:S(2)}, u32[]{:S(2)}) %all-to-all-start) | async-done | bytes 131104 | tf_op jit(solution)/shard_map/all_to_all | solution.py:337
  18.3 3.4 %all-to-all-start.1 = ((f32[32,16,128]{2,1,0:T(8,128)}), f32[32,16,128]{2,1,0:T(8,128)S(1)}, u32[]{:S(2)}, u32[]{:S(2)}) async-start(f32[32,16,128]{2,1,0:T(8,128)} %gather_rows.1), calls=%async_computation.1 | async-start | bytes 524288 | tf_op jit(solution)/shard_map/all_to_all | solution.py:347
  22.2 11.1 %phases.1 = (bf16[4,4,1024,256]{3,2,1,0:T(8,128)(2,1)}, bf16[4,4,1024,256]{3,2,1,0:T(8,128)(2,1)}, f32[8,1024]{1,0:T(8,128)}, bf16[1024,128]{1,0:T(8,128)(2,1)}) custom-call(s32[2,32]{1,0:T(2,128)S(1)} %convert_element_type.12.ends_ref, f32[4]{0:T(128)} %wave_ref.5, f32[32,8,128]{2,1,0:T(8,128)S(1)} %all-to-all-done.came_ref, ...), custom_call_target="tpu_custom_call" | custom-call | tf_op jit(solution)/shard_map/phases/pallas_call | solution.py:361
  33.4 0.7 copy-done.1
  34.1 13.6 %radiate.1 = (bf16[8,4,1024,256]{3,2,1,0:T(8,128)(2,1)S(1)}, bf16[8,4,1024,256]{3,2,1,0:T(8,128)(2,1)S(1)}, f32[8,2048]{1,0:T(8,128)S(1)}) custom-call(s32[2,32]{1,0:T(2,128)} %copy-done, f32[4]{0:T(128)} %wave_ref.5, f32[32,16,128]{2,1,0:T(8,128)} %copy-done.1, f32[8,1024]{1,0:T(8,128)} %get-tuple-element.13.rows_ref, ...), custom_call_target="tpu_custom_call" | custom-call | tf_op jit(solution)/shard_map/radiate/pallas_call | solution.py:377
  47.9 1.2 %collective-permute-done = f32[8,2048]{1,0:T(8,128)S(1)} collective-permute-done((f32[8,2048]{1,0:T(8,128)S(1)}, f32[8,2048]{1,0:T(8,128)S(1)}, u32[]{:S(2)}, u32[]{:S(2)}) %collective-permute-start) | collective-permute-done | bytes 65568 | tf_op jit(solution)/shard_map/ppermute | solution.py:312
  49.1 2.5 %collective-permute-start.3 = (f32[8,2048]{1,0:T(8,128)S(1)}, f32[8,2048]{1,0:T(8,128)S(1)}, u32[]{:S(2)}, u32[]{:S(2)}) collective-permute-start(f32[8,2048]{1,0:T(8,128)S(1)} %add.21), channel_id=1, source_target_pairs={{0,17},{1,16},{2,19},{3,18},{4,21},{5,20},{6,23},{7,22},{8,25},{9,... | collective-permute-start | bytes 196616 | tf_op jit(solution)/shard_map/ppermute | solution.py:312
  51.6 0.6 collective-permute-start.2
  52.2 0.5 collective-permute-start.1
  52.6 1.7 %collective-permute-done.3 = f32[8,2048]{1,0:T(8,128)S(1)} collective-permute-done((f32[8,2048]{1,0:T(8,128)S(1)}, f32[8,2048]{1,0:T(8,128)S(1)}, u32[]{:S(2)}, u32[]{:S(2)}) %collective-permute-start.3) | collective-permute-done | bytes 65568 | tf_op jit(solution)/shard_map/ppermute | solution.py:312
  54.3 1.6 %collective-permute-done.2 = f32[8,2048]{1,0:T(8,128)S(1)} collective-permute-done((f32[8,2048]{1,0:T(8,128)S(1)}, f32[8,2048]{1,0:T(8,128)S(1)}, u32[]{:S(2)}, u32[]{:S(2)}) %collective-permute-start.2) | collective-permute-done | bytes 65568 | tf_op jit(solution)/shard_map/ppermute | solution.py:312
  55.9 0.6 collective-permute-done.1
  56.5 3.4 %collective-permute-start.6 = (f32[8,2048]{1,0:T(8,128)S(1)}, f32[8,2048]{1,0:T(8,128)S(1)}, u32[]{:S(2)}, u32[]{:S(2)}) collective-permute-start(f32[8,2048]{1,0:T(8,128)S(1)} %add_add_fusion.rest_0_), channel_id=1, source_target_pairs={{0,6},{1,7},{2,4},{3,5},{4,2},{5,3},{6,0},{7,1},{8,14},{9,15},{10,... | collective-permute-start | bytes 196616 | tf_op jit(solution)/shard_map/ppermute | solution.py:312
  59.9 1.0 %collective-permute-start.4 = (f32[8,2048]{1,0:T(8,128)S(1)}, f32[8,2048]{1,0:T(8,128)S(1)}, u32[]{:S(2)}, u32[]{:S(2)}) collective-permute-start(f32[8,2048]{1,0:T(8,128)S(1)} %add_add_fusion.rest_0_), channel_id=1, source_target_pairs={{0,2},{1,3},{2,0},{3,1},{4,6},{5,7},{6,4},{7,5},{8,10},{9,11},{10,... | collective-permute-start | bytes 196616 | tf_op jit(solution)/shard_map/ppermute | solution.py:312
  60.9 1.8 %collective-permute-done.6.rest_3_ = f32[8,2048]{1,0:T(8,128)S(1)} collective-permute-done((f32[8,2048]{1,0:T(8,128)S(1)}, f32[8,2048]{1,0:T(8,128)S(1)}, u32[]{:S(2)}, u32[]{:S(2)}) %collective-permute-start.6) | collective-permute-done | bytes 65568 | tf_op jit(solution)/shard_map/ppermute | solution.py:312
  62.7 2.3 %collective-permute-done.5.rest_2_ = f32[8,2048]{1,0:T(8,128)S(1)} collective-permute-done((f32[8,2048]{1,0:T(8,128)S(1)}, f32[8,2048]{1,0:T(8,128)S(1)}, u32[]{:S(2)}, u32[]{:S(2)}) %collective-permute-start.5) | collective-permute-done | bytes 65568 | tf_op jit(solution)/shard_map/ppermute | solution.py:312
  65.0 10.9 %adjoint.1 = (bf16[8,4,1024,256]{3,2,1,0:T(8,128)(2,1)S(1)}, bf16[8,4,1024,256]{3,2,1,0:T(8,128)(2,1)S(1)}, f32[32,16,128]{2,1,0:T(8,128)}, f32[1]{0:T(128)}, f32[4,2,2048]{2,1,0:T(2,128)}) custom-call(s32[2,32]{1,0:T(2,128)} %copy-done, f32[4]{0:T(128)} %wave_ref.5, f32[4,2,2048]{2,1,0:T(2,128)} %target_ref.1, ...), custom_call_target="tpu_custom_call", output_to_operand_aliasing={{0}: (6, {}), {1}: (7, {})} | custom-call | tf_op jit(solution)/shard_map/adjoint/pallas_call | solution.py:399
  75.9 14.6 %all_to_all.15.value_ref = f32[32,16,128]{2,1,0:T(8,128)S(1)} all-to-all(f32[32,16,128]{2,1,0:T(8,128)} %get-tuple-element.22), channel_id=1, replica_groups=mesh['gx'=4,'gy'=8] {'gx','gy'}, dimensions={0} | all-to-all | bytes 524288 | tf_op jit(solution)/shard_map/all_to_all | solution.py:416
  90.5 2.1 %scatter_rows.1 = f32[16,8192]{1,0:T(8,128)} custom-call(f32[32,16,128]{2,1,0:T(8,128)S(1)} %all_to_all.15.value_ref, s32[32,1,128]{2,1,0:T(1,128)S(1)} %bitcast.8), custom_call_target="tpu_custom_call" | custom-call | tf_op jit(solution)/shard_map/scatter_rows/pallas_call | solution.py:417
  (17 shorter events, 0.9 us)
Async XLA Ops:
  3.2 15.0 %all-to-all-start = ((f32[32,8,128]{2,1,0:T(8,128)}), f32[32,8,128]{2,1,0:T(8,128)S(1)}, u32[]{:S(2)}, u32[]{:S(2)}) async-start(f32[32,8,128]{2,1,0:T(8,128)} %bitcast.1.rows_ref), calls=%async_computation | async-start | bytes 262144 | tf_op jit(solution)/shard_map/all_to_all | solution.py:337
  18.3 15.1 %all-to-all-start.1 = ((f32[32,16,128]{2,1,0:T(8,128)}), f32[32,16,128]{2,1,0:T(8,128)S(1)}, u32[]{:S(2)}, u32[]{:S(2)}) async-start(f32[32,16,128]{2,1,0:T(8,128)} %gather_rows.1), calls=%async_computation.1 | async-start | bytes 524288 | tf_op jit(solution)/shard_map/all_to_all | solution.py:347
  22.2 11.2 %copy-start = (s32[2,32]{1,0:T(2,128)}, s32[2,32]{1,0:T(2,128)S(1)}, u32[]{:S(2)}) copy-start(s32[2,32]{1,0:T(2,128)S(1)} %convert_element_type.12.ends_ref) | copy-start | bytes 772
  33.4 0.7 copy-start.1
  47.7 1.3 %collective-permute-start = (f32[8,2048]{1,0:T(8,128)S(1)}, f32[8,2048]{1,0:T(8,128)S(1)}, u32[]{:S(2)}, u32[]{:S(2)}) collective-permute-start(f32[8,2048]{1,0:T(8,128)S(1)} %get-tuple-element.19), channel_id=1, source_target_pairs={{0,8},{1,9},{2,10},{3,11},{4,12},{5,13},{6,14},{7,15},{8,0},{9,1},... | collective-permute-start | bytes 196616 | tf_op jit(solution)/shard_map/ppermute | solution.py:312
  49.1 5.3 %collective-permute-start.3 = (f32[8,2048]{1,0:T(8,128)S(1)}, f32[8,2048]{1,0:T(8,128)S(1)}, u32[]{:S(2)}, u32[]{:S(2)}) collective-permute-start(f32[8,2048]{1,0:T(8,128)S(1)} %add.21), channel_id=1, source_target_pairs={{0,17},{1,16},{2,19},{3,18},{4,21},{5,20},{6,23},{7,22},{8,25},{9,... | collective-permute-start | bytes 196616 | tf_op jit(solution)/shard_map/ppermute | solution.py:312
  51.6 4.3 %collective-permute-start.2 = (f32[8,2048]{1,0:T(8,128)S(1)}, f32[8,2048]{1,0:T(8,128)S(1)}, u32[]{:S(2)}, u32[]{:S(2)}) collective-permute-start(f32[8,2048]{1,0:T(8,128)S(1)} %add.21), channel_id=1, source_target_pairs={{0,16},{1,17},{2,18},{3,19},{4,20},{5,21},{6,22},{7,23},{8,24},{9,... | collective-permute-start | bytes 196616 | tf_op jit(solution)/shard_map/ppermute | solution.py:312
  52.2 4.3 %collective-permute-start.1 = (f32[8,2048]{1,0:T(8,128)S(1)}, f32[8,2048]{1,0:T(8,128)S(1)}, u32[]{:S(2)}, u32[]{:S(2)}) collective-permute-start(f32[8,2048]{1,0:T(8,128)S(1)} %add.21), channel_id=1, source_target_pairs={{0,1},{1,0},{2,3},{3,2},{4,5},{5,4},{6,7},{7,6},{8,9},{9,8},{10,11... | collective-permute-start | bytes 196616 | tf_op jit(solution)/shard_map/ppermute | solution.py:312
  56.5 6.2 %collective-permute-start.6 = (f32[8,2048]{1,0:T(8,128)S(1)}, f32[8,2048]{1,0:T(8,128)S(1)}, u32[]{:S(2)}, u32[]{:S(2)}) collective-permute-start(f32[8,2048]{1,0:T(8,128)S(1)} %add_add_fusion.rest_0_), channel_id=1, source_target_pairs={{0,6},{1,7},{2,4},{3,5},{4,2},{5,3},{6,0},{7,1},{8,14},{9,15},{10,... | collective-permute-start | bytes 196616 | tf_op jit(solution)/shard_map/ppermute | solution.py:312
  59.9 5.2 %collective-permute-start.5 = (f32[8,2048]{1,0:T(8,128)S(1)}, f32[8,2048]{1,0:T(8,128)S(1)}, u32[]{:S(2)}, u32[]{:S(2)}) collective-permute-start(f32[8,2048]{1,0:T(8,128)S(1)} %add_add_fusion.rest_0_), channel_id=1, source_target_pairs={{0,4},{1,5},{2,6},{3,7},{4,0},{5,1},{6,2},{7,3},{8,12},{9,13},{10,... | collective-permute-start | bytes 196616 | tf_op jit(solution)/shard_map/ppermute | solution.py:312
  59.9 5.2 %collective-permute-start.4 = (f32[8,2048]{1,0:T(8,128)S(1)}, f32[8,2048]{1,0:T(8,128)S(1)}, u32[]{:S(2)}, u32[]{:S(2)}) collective-permute-start(f32[8,2048]{1,0:T(8,128)S(1)} %add_add_fusion.rest_0_), channel_id=1, source_target_pairs={{0,2},{1,3},{2,0},{3,1},{4,6},{5,7},{6,4},{7,5},{8,10},{9,11},{10,... | collective-permute-start | bytes 196616 | tf_op jit(solution)/shard_map/ppermute | solution.py:312

commit v5 on v4

--- a/solution.py
+++ b/solution.py
@@ -94,10 +94,10 @@
     r = turns - jnp.round(turns)
     u = r * r
     v = u - SIN_A
-    half_sin = (v * v + SIN_B) * r
+    half_sin = ((v * v + SIN_B) * r).astype(BF16)
     w = u - COS_A
-    half_cos = w * w - COS_B
-    return (half_sin * half_sin).astype(BF16), (half_sin * half_cos).astype(BF16)
+    half_cos = (w * w - COS_B).astype(BF16)
+    return half_sin * half_sin, half_sin * half_cos
 
 
 def masked_parts(parts_ref, f):

time: 93.1 us -> 93.1 us (level)
  no operation moved by 1% of the time
where the time goes in v5:
time: 93.1 us; the launch traced here: 92.6 us
  Pallas kernels  42 us (45%)
  starting transfers between devices  18.9 us (20%)
  blocking collectives  14.6 us (16%)
  waiting for transfers between devices  11.7 us (13%)
  local copies, waits for them, and re-layouts  3.88 us (4%)
  between operations  1.38 us (1%)
    all_to_all x1, blocking collectives, on_device(): lax.all_to_all(back[:, :, :cap], AXES, split_axis=0, concat_axis=0, tiled...  14.6 us
    pallas_call x1, Pallas kernels, on_device(): pl.pallas_call(radiate_kernel, grid=(half,), in_specs=[smem(), smem(), vm...  13.6 us
    pallas_call x1, Pallas kernels, on_device(): pl.pallas_call(phase_kernel, grid=(half,), in_specs=[smem(), smem(), vmem...  11.1 us
    pallas_call x1, Pallas kernels, on_device(): pl.pallas_call(adjoint_kernel, in_specs=[smem(), smem()] + [vmem] * (6 +...  10.9 us
    ppermute x7, waiting for transfers between devices, all_sum(): lax.ppermute(x, AXES, [(i, i ^ m) for i in range(gx * gy)])  9.14 us
    ppermute x7, starting transfers between devices, all_sum(): lax.ppermute(x, AXES, [(i, i ^ m) for i in range(gx * gy)])  8.14 us
    all_to_all x1, starting transfers between devices, on_device(): came = lax.all_to_all(rows, AXES, split_axis=0, concat_axis=0, tiled=True)  7.3 us
    pallas_call x1, Pallas kernels, on_device(): pl.pallas_call(functools.partial(gather_kernel, chunk=4), in_specs=[vmem,...  4.31 us
  transfers between devices with their start and end apart: 9, of which 7 were waited for; matrix products, arithmetic and copies ran while one was open for 1% of the time, Pallas kernels for 17%

profile of v5, /device:TPU:0, one launch (start us, length us, event | category | flops | bytes accessed | tf_op | source)
XLA Modules:
  0.0 92.6 jit_solution(11741751119150877198)
XLA Ops:
  1.3 0.9 concatenate.3
  2.4 0.8 copy.16
  3.2 7.3 %all-to-all-start = ((f32[32,8,128]{2,1,0:T(8,128)}), f32[32,8,128]{2,1,0:T(8,128)S(1)}, u32[]{:S(2)}, u32[]{:S(2)}) async-start(f32[32,8,128]{2,1,0:T(8,128)} %bitcast.1.rows_ref), calls=%async_computation | async-start | bytes 262144 | tf_op jit(solution)/shard_map/all_to_all | solution.py:337
  10.5 0.8 reshape.41
  11.4 4.3 %gather_rows.1 = f32[32,16,128]{2,1,0:T(8,128)} custom-call(f32[16,8192]{1,0:T(8,128)} %cell_ref.1, s32[32,1,128]{2,1,0:T(1,128)S(1)} %bitcast.7, f32[32,8,128]{2,1,0:T(8,128)} %bitcast.1.rows_ref), custom_call_target="tpu_custom_call" | custom-call | tf_op jit(solution)/shard_map/gather_rows/pallas_call | solution.py:339
  15.7 2.6 %all-to-all-done.came_ref = f32[32,8,128]{2,1,0:T(8,128)S(1)} async-done(((f32[32,8,128]{2,1,0:T(8,128)}), f32[32,8,128]{2,1,0:T(8,128)S(1)}, u32[]{:S(2)}, u32[]{:S(2)}) %all-to-all-start) | async-done | bytes 131104 | tf_op jit(solution)/shard_map/all_to_all | solution.py:337
  18.3 3.4 %all-to-all-start.1 = ((f32[32,16,128]{2,1,0:T(8,128)}), f32[32,16,128]{2,1,0:T(8,128)S(1)}, u32[]{:S(2)}, u32[]{:S(2)}) async-start(f32[32,16,128]{2,1,0:T(8,128)} %gather_rows.1), calls=%async_computation.1 | async-start | bytes 524288 | tf_op jit(solution)/shard_map/all_to_all | solution.py:347
  22.2 11.1 %phases.1 = (bf16[4,4,1024,256]{3,2,1,0:T(8,128)(2,1)}, bf16[4,4,1024,256]{3,2,1,0:T(8,128)(2,1)}, f32[8,1024]{1,0:T(8,128)}, bf16[1024,128]{1,0:T(8,128)(2,1)}) custom-call(s32[2,32]{1,0:T(2,128)S(1)} %convert_element_type.12.ends_ref, f32[4]{0:T(128)} %wave_ref.5, f32[32,8,128]{2,1,0:T(8,128)S(1)} %all-to-all-done.came_ref, ...), custom_call_target="tpu_custom_call" | custom-call | tf_op jit(solution)/shard_map/phases/pallas_call | solution.py:361
  33.4 0.7 copy-done.1
  34.1 13.6 %radiate.1 = (bf16[8,4,1024,256]{3,2,1,0:T(8,128)(2,1)S(1)}, bf16[8,4,1024,256]{3,2,1,0:T(8,128)(2,1)S(1)}, f32[8,2048]{1,0:T(8,128)S(1)}) custom-call(s32[2,32]{1,0:T(2,128)} %copy-done, f32[4]{0:T(128)} %wave_ref.5, f32[32,16,128]{2,1,0:T(8,128)} %copy-done.1, f32[8,1024]{1,0:T(8,128)} %get-tuple-element.13.rows_ref, ...), custom_call_target="tpu_custom_call" | custom-call | tf_op jit(solution)/shard_map/radiate/pallas_call | solution.py:377
  47.8 1.2 %collective-permute-done = f32[8,2048]{1,0:T(8,128)S(1)} collective-permute-done((f32[8,2048]{1,0:T(8,128)S(1)}, f32[8,2048]{1,0:T(8,128)S(1)}, u32[]{:S(2)}, u32[]{:S(2)}) %collective-permute-start) | collective-permute-done | bytes 65568 | tf_op jit(solution)/shard_map/ppermute | solution.py:312
  49.0 2.6 %collective-permute-start.3 = (f32[8,2048]{1,0:T(8,128)S(1)}, f32[8,2048]{1,0:T(8,128)S(1)}, u32[]{:S(2)}, u32[]{:S(2)}) collective-permute-start(f32[8,2048]{1,0:T(8,128)S(1)} %add.21), channel_id=1, source_target_pairs={{0,17},{1,16},{2,19},{3,18},{4,21},{5,20},{6,23},{7,22},{8,25},{9,... | collective-permute-start | bytes 196616 | tf_op jit(solution)/shard_map/ppermute | solution.py:312
  51.6 0.6 collective-permute-start.2
  52.1 0.4 collective-permute-start.1
  52.5 1.7 %collective-permute-done.3 = f32[8,2048]{1,0:T(8,128)S(1)} collective-permute-done((f32[8,2048]{1,0:T(8,128)S(1)}, f32[8,2048]{1,0:T(8,128)S(1)}, u32[]{:S(2)}, u32[]{:S(2)}) %collective-permute-start.3) | collective-permute-done | bytes 65568 | tf_op jit(solution)/shard_map/ppermute | solution.py:312
  54.2 1.6 %collective-permute-done.2 = f32[8,2048]{1,0:T(8,128)S(1)} collective-permute-done((f32[8,2048]{1,0:T(8,128)S(1)}, f32[8,2048]{1,0:T(8,128)S(1)}, u32[]{:S(2)}, u32[]{:S(2)}) %collective-permute-start.2) | collective-permute-done | bytes 65568 | tf_op jit(solution)/shard_map/ppermute | solution.py:312
  55.8 0.6 collective-permute-done.1
  56.4 3.4 %collective-permute-start.6 = (f32[8,2048]{1,0:T(8,128)S(1)}, f32[8,2048]{1,0:T(8,128)S(1)}, u32[]{:S(2)}, u32[]{:S(2)}) collective-permute-start(f32[8,2048]{1,0:T(8,128)S(1)} %add_add_fusion.rest_0_), channel_id=1, source_target_pairs={{0,6},{1,7},{2,4},{3,5},{4,2},{5,3},{6,0},{7,1},{8,14},{9,15},{10,... | collective-permute-start | bytes 196616 | tf_op jit(solution)/shard_map/ppermute | solution.py:312
  59.8 1.0 %collective-permute-start.4 = (f32[8,2048]{1,0:T(8,128)S(1)}, f32[8,2048]{1,0:T(8,128)S(1)}, u32[]{:S(2)}, u32[]{:S(2)}) collective-permute-start(f32[8,2048]{1,0:T(8,128)S(1)} %add_add_fusion.rest_0_), channel_id=1, source_target_pairs={{0,2},{1,3},{2,0},{3,1},{4,6},{5,7},{6,4},{7,5},{8,10},{9,11},{10,... | collective-permute-start | bytes 196616 | tf_op jit(solution)/shard_map/ppermute | solution.py:312
  60.9 1.8 %collective-permute-done.6.rest_3_ = f32[8,2048]{1,0:T(8,128)S(1)} collective-permute-done((f32[8,2048]{1,0:T(8,128)S(1)}, f32[8,2048]{1,0:T(8,128)S(1)}, u32[]{:S(2)}, u32[]{:S(2)}) %collective-permute-start.6) | collective-permute-done | bytes 65568 | tf_op jit(solution)/shard_map/ppermute | solution.py:312
  62.6 2.4 %collective-permute-done.5.rest_2_ = f32[8,2048]{1,0:T(8,128)S(1)} collective-permute-done((f32[8,2048]{1,0:T(8,128)S(1)}, f32[8,2048]{1,0:T(8,128)S(1)}, u32[]{:S(2)}, u32[]{:S(2)}) %collective-permute-start.5) | collective-permute-done | bytes 65568 | tf_op jit(solution)/shard_map/ppermute | solution.py:312
  65.0 10.9 %adjoint.1 = (bf16[8,4,1024,256]{3,2,1,0:T(8,128)(2,1)S(1)}, bf16[8,4,1024,256]{3,2,1,0:T(8,128)(2,1)S(1)}, f32[32,16,128]{2,1,0:T(8,128)}, f32[1]{0:T(128)}, f32[4,2,2048]{2,1,0:T(2,128)}) custom-call(s32[2,32]{1,0:T(2,128)} %copy-done, f32[4]{0:T(128)} %wave_ref.5, f32[4,2,2048]{2,1,0:T(2,128)} %target_ref.1, ...), custom_call_target="tpu_custom_call", output_to_operand_aliasing={{0}: (6, {}), {1}: (7, {})} | custom-call | tf_op jit(solution)/shard_map/adjoint/pallas_call | solution.py:399
  75.9 14.6 %all_to_all.15.value_ref = f32[32,16,128]{2,1,0:T(8,128)S(1)} all-to-all(f32[32,16,128]{2,1,0:T(8,128)} %get-tuple-element.22), channel_id=1, replica_groups=mesh['gx'=4,'gy'=8] {'gx','gy'}, dimensions={0} | all-to-all | bytes 524288 | tf_op jit(solution)/shard_map/all_to_all | solution.py:416
  90.5 2.1 %scatter_rows.1 = f32[16,8192]{1,0:T(8,128)} custom-call(f32[32,16,128]{2,1,0:T(8,128)S(1)} %all_to_all.15.value_ref, s32[32,1,128]{2,1,0:T(1,128)S(1)} %bitcast.8), custom_call_target="tpu_custom_call" | custom-call | tf_op jit(solution)/shard_map/scatter_rows/pallas_call | solution.py:417
  (17 shorter events, 0.9 us)
Async XLA Ops:
  3.2 15.0 %all-to-all-start = ((f32[32,8,128]{2,1,0:T(8,128)}), f32[32,8,128]{2,1,0:T(8,128)S(1)}, u32[]{:S(2)}, u32[]{:S(2)}) async-start(f32[32,8,128]{2,1,0:T(8,128)} %bitcast.1.rows_ref), calls=%async_computation | async-start | bytes 262144 | tf_op jit(solution)/shard_map/all_to_all | solution.py:337
  18.3 15.1 %all-to-all-start.1 = ((f32[32,16,128]{2,1,0:T(8,128)}), f32[32,16,128]{2,1,0:T(8,128)S(1)}, u32[]{:S(2)}, u32[]{:S(2)}) async-start(f32[32,16,128]{2,1,0:T(8,128)} %gather_rows.1), calls=%async_computation.1 | async-start | bytes 524288 | tf_op jit(solution)/shard_map/all_to_all | solution.py:347
  22.2 11.1 %copy-start = (s32[2,32]{1,0:T(2,128)}, s32[2,32]{1,0:T(2,128)S(1)}, u32[]{:S(2)}) copy-start(s32[2,32]{1,0:T(2,128)S(1)} %convert_element_type.12.ends_ref) | copy-start | bytes 772
  33.4 0.7 copy-start.1
  47.7 1.3 %collective-permute-start = (f32[8,2048]{1,0:T(8,128)S(1)}, f32[8,2048]{1,0:T(8,128)S(1)}, u32[]{:S(2)}, u32[]{:S(2)}) collective-permute-start(f32[8,2048]{1,0:T(8,128)S(1)} %get-tuple-element.19), channel_id=1, source_target_pairs={{0,8},{1,9},{2,10},{3,11},{4,12},{5,13},{6,14},{7,15},{8,0},{9,1},... | collective-permute-start | bytes 196616 | tf_op jit(solution)/shard_map/ppermute | solution.py:312
  49.0 5.2 %collective-permute-start.3 = (f32[8,2048]{1,0:T(8,128)S(1)}, f32[8,2048]{1,0:T(8,128)S(1)}, u32[]{:S(2)}, u32[]{:S(2)}) collective-permute-start(f32[8,2048]{1,0:T(8,128)S(1)} %add.21), channel_id=1, source_target_pairs={{0,17},{1,16},{2,19},{3,18},{4,21},{5,20},{6,23},{7,22},{8,25},{9,... | collective-permute-start | bytes 196616 | tf_op jit(solution)/shard_map/ppermute | solution.py:312
  51.6 4.3 %collective-permute-start.2 = (f32[8,2048]{1,0:T(8,128)S(1)}, f32[8,2048]{1,0:T(8,128)S(1)}, u32[]{:S(2)}, u32[]{:S(2)}) collective-permute-start(f32[8,2048]{1,0:T(8,128)S(1)} %add.21), channel_id=1, source_target_pairs={{0,16},{1,17},{2,18},{3,19},{4,20},{5,21},{6,22},{7,23},{8,24},{9,... | collective-permute-start | bytes 196616 | tf_op jit(solution)/shard_map/ppermute | solution.py:312
  52.1 4.3 %collective-permute-start.1 = (f32[8,2048]{1,0:T(8,128)S(1)}, f32[8,2048]{1,0:T(8,128)S(1)}, u32[]{:S(2)}, u32[]{:S(2)}) collective-permute-start(f32[8,2048]{1,0:T(8,128)S(1)} %add.21), channel_id=1, source_target_pairs={{0,1},{1,0},{2,3},{3,2},{4,5},{5,4},{6,7},{7,6},{8,9},{9,8},{10,11... | collective-permute-start | bytes 196616 | tf_op jit(solution)/shard_map/ppermute | solution.py:312
  56.4 6.2 %collective-permute-start.6 = (f32[8,2048]{1,0:T(8,128)S(1)}, f32[8,2048]{1,0:T(8,128)S(1)}, u32[]{:S(2)}, u32[]{:S(2)}) collective-permute-start(f32[8,2048]{1,0:T(8,128)S(1)} %add_add_fusion.rest_0_), channel_id=1, source_target_pairs={{0,6},{1,7},{2,4},{3,5},{4,2},{5,3},{6,0},{7,1},{8,14},{9,15},{10,... | collective-permute-start | bytes 196616 | tf_op jit(solution)/shard_map/ppermute | solution.py:312
  59.8 5.2 %collective-permute-start.5 = (f32[8,2048]{1,0:T(8,128)S(1)}, f32[8,2048]{1,0:T(8,128)S(1)}, u32[]{:S(2)}, u32[]{:S(2)}) collective-permute-start(f32[8,2048]{1,0:T(8,128)S(1)} %add_add_fusion.rest_0_), channel_id=1, source_target_pairs={{0,4},{1,5},{2,6},{3,7},{4,0},{5,1},{6,2},{7,3},{8,12},{9,13},{10,... | collective-permute-start | bytes 196616 | tf_op jit(solution)/shard_map/ppermute | solution.py:312
  59.8 5.2 %collective-permute-start.4 = (f32[8,2048]{1,0:T(8,128)S(1)}, f32[8,2048]{1,0:T(8,128)S(1)}, u32[]{:S(2)}, u32[]{:S(2)}) collective-permute-start(f32[8,2048]{1,0:T(8,128)S(1)} %add_add_fusion.rest_0_), channel_id=1, source_target_pairs={{0,2},{1,3},{2,0},{3,1},{4,6},{5,7},{6,4},{7,5},{8,10},{9,11},{10,... | collective-permute-start | bytes 196616 | tf_op jit(solution)/shard_map/ppermute | solution.py:312

commit v6 on v4

--- a/solution.py
+++ b/solution.py
@@ -86,7 +86,7 @@
         pltpu.store(packed_ref.at[base + 1], tile, mask=lane < shift)
         return carry
 
-    lax.fori_loop(0, sources, body, 0, unroll=8)
+    lax.fori_loop(0, sources, body, 0, unroll=32)
     return jnp.concatenate([packed_ref[b] for b in range(packed_ref.shape[0] - 1)], axis=1)
 
 
@@ -243,7 +243,7 @@
         out_ref[s] = jnp.where(lane < ends_ref[1, s], joined, 0.0)
         return carry
 
-    lax.fori_loop(0, out_ref.shape[0], body, 0, unroll=8)
+    lax.fori_loop(0, out_ref.shape[0], body, 0, unroll=32)
 
 
 def scatter_kernel(value_ref, index_ref, out_ref, *, chunk):

time: 93.1 us -> 92.6 us (level)
  no operation moved by 1% of the time
where the time goes in v6:
time: 92.6 us; the launch traced here: 92.1 us
  Pallas kernels  41.6 us (45%)
  starting transfers between devices  18.9 us (20%)
  blocking collectives  14.6 us (16%)
  waiting for transfers between devices  11.7 us (13%)
  local copies, waits for them, and re-layouts  3.88 us (4%)
  between operations  1.38 us (1%)
    all_to_all x1, blocking collectives, on_device(): lax.all_to_all(back[:, :, :cap], AXES, split_axis=0, concat_axis=0, tiled...  14.6 us
    pallas_call x1, Pallas kernels, on_device(): pl.pallas_call(radiate_kernel, grid=(half,), in_specs=[smem(), smem(), vm...  13.5 us
    pallas_call x1, Pallas kernels, on_device(): pl.pallas_call(phase_kernel, grid=(half,), in_specs=[smem(), smem(), vmem...  11 us
    pallas_call x1, Pallas kernels, on_device(): pl.pallas_call(adjoint_kernel, in_specs=[smem(), smem()] + [vmem] * (6 +...  10.7 us
    ppermute x7, waiting for transfers between devices, all_sum(): lax.ppermute(x, AXES, [(i, i ^ m) for i in range(gx * gy)])  9.12 us
    ppermute x7, starting transfers between devices, all_sum(): lax.ppermute(x, AXES, [(i, i ^ m) for i in range(gx * gy)])  8.15 us
    all_to_all x1, starting transfers between devices, on_device(): came = lax.all_to_all(rows, AXES, split_axis=0, concat_axis=0, tiled=True)  7.3 us
    pallas_call x1, Pallas kernels, on_device(): pl.pallas_call(functools.partial(gather_kernel, chunk=4), in_specs=[vmem,...  4.31 us
  transfers between devices with their start and end apart: 9, of which 7 were waited for; matrix products, arithmetic and copies ran while one was open for 1% of the time, Pallas kernels for 17%

profile of v6, /device:TPU:0, one launch (start us, length us, event | category | flops | bytes accessed | tf_op | source)
XLA Modules:
  0.0 92.1 jit_solution(12589996109331134712)
XLA Ops:
  1.3 0.9 concatenate.3
  2.4 0.8 copy.16
  3.2 7.3 %all-to-all-start = ((f32[32,8,128]{2,1,0:T(8,128)}), f32[32,8,128]{2,1,0:T(8,128)S(1)}, u32[]{:S(2)}, u32[]{:S(2)}) async-start(f32[32,8,128]{2,1,0:T(8,128)} %bitcast.1.rows_ref), calls=%async_computation | async-start | bytes 262144 | tf_op jit(solution)/shard_map/all_to_all | solution.py:337
  10.5 0.8 reshape.41
  11.4 4.3 %gather_rows.1 = f32[32,16,128]{2,1,0:T(8,128)} custom-call(f32[16,8192]{1,0:T(8,128)} %cell_ref.1, s32[32,1,128]{2,1,0:T(1,128)S(1)} %bitcast.7, f32[32,8,128]{2,1,0:T(8,128)} %bitcast.1.rows_ref), custom_call_target="tpu_custom_call" | custom-call | tf_op jit(solution)/shard_map/gather_rows/pallas_call | solution.py:339
  15.7 2.6 %all-to-all-done.came_ref = f32[32,8,128]{2,1,0:T(8,128)S(1)} async-done(((f32[32,8,128]{2,1,0:T(8,128)}), f32[32,8,128]{2,1,0:T(8,128)S(1)}, u32[]{:S(2)}, u32[]{:S(2)}) %all-to-all-start) | async-done | bytes 131104 | tf_op jit(solution)/shard_map/all_to_all | solution.py:337
  18.3 3.4 %all-to-all-start.1 = ((f32[32,16,128]{2,1,0:T(8,128)}), f32[32,16,128]{2,1,0:T(8,128)S(1)}, u32[]{:S(2)}, u32[]{:S(2)}) async-start(f32[32,16,128]{2,1,0:T(8,128)} %gather_rows.1), calls=%async_computation.1 | async-start | bytes 524288 | tf_op jit(solution)/shard_map/all_to_all | solution.py:347
  22.2 11.0 %phases.1 = (bf16[4,4,1024,256]{3,2,1,0:T(8,128)(2,1)}, bf16[4,4,1024,256]{3,2,1,0:T(8,128)(2,1)}, f32[8,1024]{1,0:T(8,128)}, bf16[1024,128]{1,0:T(8,128)(2,1)}) custom-call(s32[2,32]{1,0:T(2,128)S(1)} %convert_element_type.12.ends_ref, f32[4]{0:T(128)} %wave_ref.5, f32[32,8,128]{2,1,0:T(8,128)S(1)} %all-to-all-done.came_ref, ...), custom_call_target="tpu_custom_call" | custom-call | tf_op jit(solution)/shard_map/phases/pallas_call | solution.py:361
  33.3 0.7 copy-done.1
  34.0 13.5 %radiate.1 = (bf16[8,4,1024,256]{3,2,1,0:T(8,128)(2,1)S(1)}, bf16[8,4,1024,256]{3,2,1,0:T(8,128)(2,1)S(1)}, f32[8,2048]{1,0:T(8,128)S(1)}) custom-call(s32[2,32]{1,0:T(2,128)} %copy-done, f32[4]{0:T(128)} %wave_ref.5, f32[32,16,128]{2,1,0:T(8,128)} %copy-done.1, f32[8,1024]{1,0:T(8,128)} %get-tuple-element.13.rows_ref, ...), custom_call_target="tpu_custom_call" | custom-call | tf_op jit(solution)/shard_map/radiate/pallas_call | solution.py:377
  47.6 1.2 %collective-permute-done = f32[8,2048]{1,0:T(8,128)S(1)} collective-permute-done((f32[8,2048]{1,0:T(8,128)S(1)}, f32[8,2048]{1,0:T(8,128)S(1)}, u32[]{:S(2)}, u32[]{:S(2)}) %collective-permute-start) | collective-permute-done | bytes 65568 | tf_op jit(solution)/shard_map/ppermute | solution.py:312
  48.8 2.6 %collective-permute-start.3 = (f32[8,2048]{1,0:T(8,128)S(1)}, f32[8,2048]{1,0:T(8,128)S(1)}, u32[]{:S(2)}, u32[]{:S(2)}) collective-permute-start(f32[8,2048]{1,0:T(8,128)S(1)} %add.21), channel_id=1, source_target_pairs={{0,17},{1,16},{2,19},{3,18},{4,21},{5,20},{6,23},{7,22},{8,25},{9,... | collective-permute-start | bytes 196616 | tf_op jit(solution)/shard_map/ppermute | solution.py:312
  51.4 0.6 collective-permute-start.2
  51.9 0.4 collective-permute-start.1
  52.4 1.7 %collective-permute-done.3 = f32[8,2048]{1,0:T(8,128)S(1)} collective-permute-done((f32[8,2048]{1,0:T(8,128)S(1)}, f32[8,2048]{1,0:T(8,128)S(1)}, u32[]{:S(2)}, u32[]{:S(2)}) %collective-permute-start.3) | collective-permute-done | bytes 65568 | tf_op jit(solution)/shard_map/ppermute | solution.py:312
  54.0 1.6 %collective-permute-done.2 = f32[8,2048]{1,0:T(8,128)S(1)} collective-permute-done((f32[8,2048]{1,0:T(8,128)S(1)}, f32[8,2048]{1,0:T(8,128)S(1)}, u32[]{:S(2)}, u32[]{:S(2)}) %collective-permute-start.2) | collective-permute-done | bytes 65568 | tf_op jit(solution)/shard_map/ppermute | solution.py:312
  55.6 0.6 collective-permute-done.1
  56.2 3.4 %collective-permute-start.6 = (f32[8,2048]{1,0:T(8,128)S(1)}, f32[8,2048]{1,0:T(8,128)S(1)}, u32[]{:S(2)}, u32[]{:S(2)}) collective-permute-start(f32[8,2048]{1,0:T(8,128)S(1)} %add_add_fusion.rest_0_), channel_id=1, source_target_pairs={{0,6},{1,7},{2,4},{3,5},{4,2},{5,3},{6,0},{7,1},{8,14},{9,15},{10,... | collective-permute-start | bytes 196616 | tf_op jit(solution)/shard_map/ppermute | solution.py:312
  59.6 1.0 %collective-permute-start.4 = (f32[8,2048]{1,0:T(8,128)S(1)}, f32[8,2048]{1,0:T(8,128)S(1)}, u32[]{:S(2)}, u32[]{:S(2)}) collective-permute-start(f32[8,2048]{1,0:T(8,128)S(1)} %add_add_fusion.rest_0_), channel_id=1, source_target_pairs={{0,2},{1,3},{2,0},{3,1},{4,6},{5,7},{6,4},{7,5},{8,10},{9,11},{10,... | collective-permute-start | bytes 196616 | tf_op jit(solution)/shard_map/ppermute | solution.py:312
  60.7 1.8 %collective-permute-done.6.rest_3_ = f32[8,2048]{1,0:T(8,128)S(1)} collective-permute-done((f32[8,2048]{1,0:T(8,128)S(1)}, f32[8,2048]{1,0:T(8,128)S(1)}, u32[]{:S(2)}, u32[]{:S(2)}) %collective-permute-start.6) | collective-permute-done | bytes 65568 | tf_op jit(solution)/shard_map/ppermute | solution.py:312
  62.4 2.3 %collective-permute-done.5.rest_2_ = f32[8,2048]{1,0:T(8,128)S(1)} collective-permute-done((f32[8,2048]{1,0:T(8,128)S(1)}, f32[8,2048]{1,0:T(8,128)S(1)}, u32[]{:S(2)}, u32[]{:S(2)}) %collective-permute-start.5) | collective-permute-done | bytes 65568 | tf_op jit(solution)/shard_map/ppermute | solution.py:312
  64.8 10.7 %adjoint.1 = (bf16[8,4,1024,256]{3,2,1,0:T(8,128)(2,1)S(1)}, bf16[8,4,1024,256]{3,2,1,0:T(8,128)(2,1)S(1)}, f32[32,16,128]{2,1,0:T(8,128)}, f32[1]{0:T(128)}, f32[4,2,2048]{2,1,0:T(2,128)}) custom-call(s32[2,32]{1,0:T(2,128)} %copy-done, f32[4]{0:T(128)} %wave_ref.5, f32[4,2,2048]{2,1,0:T(2,128)} %target_ref.1, ...), custom_call_target="tpu_custom_call", output_to_operand_aliasing={{0}: (6, {}), {1}: (7, {})} | custom-call | tf_op jit(solution)/shard_map/adjoint/pallas_call | solution.py:399
  75.5 14.6 %all_to_all.15.value_ref = f32[32,16,128]{2,1,0:T(8,128)S(1)} all-to-all(f32[32,16,128]{2,1,0:T(8,128)} %get-tuple-element.22), channel_id=1, replica_groups=mesh['gx'=4,'gy'=8] {'gx','gy'}, dimensions={0} | all-to-all | bytes 524288 | tf_op jit(solution)/shard_map/all_to_all | solution.py:416
  90.1 2.1 %scatter_rows.1 = f32[16,8192]{1,0:T(8,128)} custom-call(f32[32,16,128]{2,1,0:T(8,128)S(1)} %all_to_all.15.value_ref, s32[32,1,128]{2,1,0:T(1,128)S(1)} %bitcast.8), custom_call_target="tpu_custom_call" | custom-call | tf_op jit(solution)/shard_map/scatter_rows/pallas_call | solution.py:417
  (17 shorter events, 0.9 us)
Async XLA Ops:
  3.2 15.0 %all-to-all-start = ((f32[32,8,128]{2,1,0:T(8,128)}), f32[32,8,128]{2,1,0:T(8,128)S(1)}, u32[]{:S(2)}, u32[]{:S(2)}) async-start(f32[32,8,128]{2,1,0:T(8,128)} %bitcast.1.rows_ref), calls=%async_computation | async-start | bytes 262144 | tf_op jit(solution)/shard_map/all_to_all | solution.py:337
  18.3 15.0 %all-to-all-start.1 = ((f32[32,16,128]{2,1,0:T(8,128)}), f32[32,16,128]{2,1,0:T(8,128)S(1)}, u32[]{:S(2)}, u32[]{:S(2)}) async-start(f32[32,16,128]{2,1,0:T(8,128)} %gather_rows.1), calls=%async_computation.1 | async-start | bytes 524288 | tf_op jit(solution)/shard_map/all_to_all | solution.py:347
  22.2 11.0 %copy-start = (s32[2,32]{1,0:T(2,128)}, s32[2,32]{1,0:T(2,128)S(1)}, u32[]{:S(2)}) copy-start(s32[2,32]{1,0:T(2,128)S(1)} %convert_element_type.12.ends_ref) | copy-start | bytes 772
  33.3 0.7 copy-start.1
  47.5 1.3 %collective-permute-start = (f32[8,2048]{1,0:T(8,128)S(1)}, f32[8,2048]{1,0:T(8,128)S(1)}, u32[]{:S(2)}, u32[]{:S(2)}) collective-permute-start(f32[8,2048]{1,0:T(8,128)S(1)} %get-tuple-element.19), channel_id=1, source_target_pairs={{0,8},{1,9},{2,10},{3,11},{4,12},{5,13},{6,14},{7,15},{8,0},{9,1},... | collective-permute-start | bytes 196616 | tf_op jit(solution)/shard_map/ppermute | solution.py:312
  48.8 5.2 %collective-permute-start.3 = (f32[8,2048]{1,0:T(8,128)S(1)}, f32[8,2048]{1,0:T(8,128)S(1)}, u32[]{:S(2)}, u32[]{:S(2)}) collective-permute-start(f32[8,2048]{1,0:T(8,128)S(1)} %add.21), channel_id=1, source_target_pairs={{0,17},{1,16},{2,19},{3,18},{4,21},{5,20},{6,23},{7,22},{8,25},{9,... | collective-permute-start | bytes 196616 | tf_op jit(solution)/shard_map/ppermute | solution.py:312
  51.4 4.3 %collective-permute-start.2 = (f32[8,2048]{1,0:T(8,128)S(1)}, f32[8,2048]{1,0:T(8,128)S(1)}, u32[]{:S(2)}, u32[]{:S(2)}) collective-permute-start(f32[8,2048]{1,0:T(8,128)S(1)} %add.21), channel_id=1, source_target_pairs={{0,16},{1,17},{2,18},{3,19},{4,20},{5,21},{6,22},{7,23},{8,24},{9,... | collective-permute-start | bytes 196616 | tf_op jit(solution)/shard_map/ppermute | solution.py:312
  51.9 4.3 %collective-permute-start.1 = (f32[8,2048]{1,0:T(8,128)S(1)}, f32[8,2048]{1,0:T(8,128)S(1)}, u32[]{:S(2)}, u32[]{:S(2)}) collective-permute-start(f32[8,2048]{1,0:T(8,128)S(1)} %add.21), channel_id=1, source_target_pairs={{0,1},{1,0},{2,3},{3,2},{4,5},{5,4},{6,7},{7,6},{8,9},{9,8},{10,11... | collective-permute-start | bytes 196616 | tf_op jit(solution)/shard_map/ppermute | solution.py:312
  56.2 6.2 %collective-permute-start.6 = (f32[8,2048]{1,0:T(8,128)S(1)}, f32[8,2048]{1,0:T(8,128)S(1)}, u32[]{:S(2)}, u32[]{:S(2)}) collective-permute-start(f32[8,2048]{1,0:T(8,128)S(1)} %add_add_fusion.rest_0_), channel_id=1, source_target_pairs={{0,6},{1,7},{2,4},{3,5},{4,2},{5,3},{6,0},{7,1},{8,14},{9,15},{10,... | collective-permute-start | bytes 196616 | tf_op jit(solution)/shard_map/ppermute | solution.py:312
  59.6 5.2 %collective-permute-start.5 = (f32[8,2048]{1,0:T(8,128)S(1)}, f32[8,2048]{1,0:T(8,128)S(1)}, u32[]{:S(2)}, u32[]{:S(2)}) collective-permute-start(f32[8,2048]{1,0:T(8,128)S(1)} %add_add_fusion.rest_0_), channel_id=1, source_target_pairs={{0,4},{1,5},{2,6},{3,7},{4,0},{5,1},{6,2},{7,3},{8,12},{9,13},{10,... | collective-permute-start | bytes 196616 | tf_op jit(solution)/shard_map/ppermute | solution.py:312
  59.6 5.2 %collective-permute-start.4 = (f32[8,2048]{1,0:T(8,128)S(1)}, f32[8,2048]{1,0:T(8,128)S(1)}, u32[]{:S(2)}, u32[]{:S(2)}) collective-permute-start(f32[8,2048]{1,0:T(8,128)S(1)} %add_add_fusion.rest_0_), channel_id=1, source_target_pairs={{0,2},{1,3},{2,0},{3,1},{4,6},{5,7},{6,4},{7,5},{8,10},{9,11},{10,... | collective-permute-start | bytes 196616 | tf_op jit(solution)/shard_map/ppermute | solution.py:312

commit v7 on v6

--- a/solution.py
+++ b/solution.py
@@ -100,8 +100,7 @@
     return (half_sin * half_sin).astype(BF16), (half_sin * half_cos).astype(BF16)
 
 
-def masked_parts(parts_ref, f):
-    parts = parts_ref[...]
+def masked_parts(parts, f):
     level = lax.broadcasted_iota(jnp.int32, parts.shape, 0)
     return jnp.where((level >= 32 * f) & (level < 32 * f + 32), parts.astype(F32), 0.0).astype(BF16)
 
@@ -120,7 +119,7 @@
         y_ref[...] = jnp.concatenate(turned, axis=0).T.astype(BF16)
 
     for f in range(FREQS):
-        parts = masked_parts(parts_ref, f)
+        parts = masked_parts(parts_ref[...], f)
         for i in range(live_own // PIECE):
             at = slice(i * PIECE, (i + 1) * PIECE)
             turns = jnp.dot(y_ref[at, :], parts, preferred_element_type=F32)
@@ -129,11 +128,11 @@
 
 def radiate_kernel(
     ends_ref, wave_ref, came_ref, rows_ref, y_ref, parts_ref, basis_ref, first_t_ref, first_s_ref,
-    t_ref, s_ref, far_ref, packed_ref, src_ref, t_sem, s_sem,
+    t_ref, s_ref, far_ref, packed_ref, src_ref, t_sem, s_sem, *, half_steps,
 ):
     live_own = rows_ref.shape[1]
     step = pl.program_id(0)
-    steps = pl.num_programs(0)
+    steps = half_steps
     half, _, _, width = first_t_ref.shape
 
     def fetch(i):
@@ -163,27 +162,34 @@
         imag_z = jnp.sum(weighted[4:8], axis=0, keepdims=True)
         return [imag_z * (-wave_ref[f]), real_z * wave_ref[f]]
 
-    first, second = (pl.ds(pl.multiple_of(i * width, width), width) for i in (step, steps + step))
-    basis1 = basis_ref[0:4, first]
-    basis2 = basis_ref[0:4, second]
-    far1, far2 = [], []
-    for f in range(FREQS):
-        parts = masked_parts(parts_ref, f)
-        for i in range(live_own // PIECE):
-            at = slice(i * PIECE, (i + 1) * PIECE)
-            turns = jnp.dot(y_ref[at, :], parts, preferred_element_type=F32)
-            t_ref[steps + step, f, at, :], s_ref[steps + step, f, at, :] = half_angle(turns)
-        total_t = jnp.dot(src_ref[f, 0], t_ref[steps + step, f], preferred_element_type=F32)
-        total_s = jnp.dot(src_ref[f, 1], s_ref[steps + step, f], preferred_element_type=F32)
-        far2 += project(f, total_t, total_s, basis2)
-    for copy in fetch(step):
-        copy.wait()
-    for f in range(FREQS):
-        total_t = jnp.dot(src_ref[f, 0], t_ref[step, f], preferred_element_type=F32)
-        total_s = jnp.dot(src_ref[f, 1], s_ref[step, f], preferred_element_type=F32)
-        far1 += project(f, total_t, total_s, basis1)
-    far_ref[:, first] = jnp.concatenate(far1, axis=0)
-    far_ref[:, second] = jnp.concatenate(far2, axis=0)
+    per = half // steps
+    for j in range(per):
+        tile = step * per + j
+        at = pl.ds(pl.multiple_of((half + tile) * width, width), width)
+        basis = basis_ref[0:4, at]
+        far = []
+        for f in range(FREQS):
+            parts = masked_parts(parts_ref[:, j * width : (j + 1) * width], f)
+            turns = jnp.dot(y_ref[...], parts, preferred_element_type=F32)
+            t_ref[half + tile, f], s_ref[half + tile, f] = half_angle(turns)
+            total_t = jnp.dot(src_ref[f, 0], t_ref[half + tile, f], preferred_element_type=F32)
+            total_s = jnp.dot(src_ref[f, 1], s_ref[half + tile, f], preferred_element_type=F32)
+            far += project(f, total_t, total_s, basis)
+        far_ref[:, at] = jnp.concatenate(far, axis=0)
+    for j in range(per):
+        tile = step * per + j
+        for copy in fetch(tile):
+            copy.wait()
+    for j in range(per):
+        tile = step * per + j
+        at = pl.ds(pl.multiple_of(tile * width, width), width)
+        basis = basis_ref[0:4, at]
+        far = []
+        for f in range(FREQS):
+            total_t = jnp.dot(src_ref[f, 0], t_ref[tile, f], preferred_element_type=F32)
+            total_s = jnp.dot(src_ref[f, 1], s_ref[tile, f], preferred_element_type=F32)
+            far += project(f, total_t, total_s, basis)
+        far_ref[:, at] = jnp.concatenate(far, axis=0)
 
 
 def adjoint_kernel(
@@ -375,11 +381,11 @@
 
     hbm = pl.BlockSpec(memory_space=pltpu.HBM)
     t_all, s_all, far = pl.pallas_call(
-        radiate_kernel,
-        grid=(half,),
+        functools.partial(radiate_kernel, half_steps=half // 4),
+        grid=(half // 4,),
         in_specs=[
             smem(), smem(), vmem, vmem, vmem,
-            pl.BlockSpec((32 * FREQS, width), lambda i: (0, half + i)),
+            pl.BlockSpec((32 * FREQS, 4 * width), lambda i: (0, half // 4 + i)),
             vmem, hbm, hbm,
         ],
         out_specs=[vmem] * 3,

time: 92.6 us -> 91.1 us (0.984)
  Pallas kernels: 41.6 us -> 40 us
    pallas_call x1, Pallas kernels: 13.5 us -> 11.7 us  [on_device(): pl.pallas_call(functools.partial(radiate_kernel, half_steps=half // 4), g...]
  transfers between devices with their start and end apart: 9 -> 9, of which waited for: 7 -> 7; matrix products, arithmetic and copies ran while one was open for 1% -> 2% of each run, Pallas kernels for 17% -> 17%
where the time goes in v7:
time: 91.1 us; the launch traced here: 90.6 us
  Pallas kernels  40 us (44%)
  starting transfers between devices  18.9 us (21%)
  blocking collectives  14.6 us (16%)
  waiting for transfers between devices  11.7 us (13%)
  local copies, waits for them, and re-layouts  3.88 us (4%)
  between operations  1.39 us (2%)
    all_to_all x1, blocking collectives, on_device(): lax.all_to_all(back[:, :, :cap], AXES, split_axis=0, concat_axis=0, tiled...  14.6 us
    pallas_call x1, Pallas kernels, on_device(): pl.pallas_call(functools.partial(radiate_kernel, half_steps=half // 4), g...  11.7 us
    pallas_call x1, Pallas kernels, on_device(): pl.pallas_call(phase_kernel, grid=(half,), in_specs=[smem(), smem(), vmem...  11 us
    pallas_call x1, Pallas kernels, on_device(): pl.pallas_call(adjoint_kernel, in_specs=[smem(), smem()] + [vmem] * (6 +...  10.9 us
    ppermute x7, waiting for transfers between devices, all_sum(): lax.ppermute(x, AXES, [(i, i ^ m) for i in range(gx * gy)])  9.12 us
    ppermute x7, starting transfers between devices, all_sum(): lax.ppermute(x, AXES, [(i, i ^ m) for i in range(gx * gy)])  8.33 us
    all_to_all x1, starting transfers between devices, on_device(): came = lax.all_to_all(rows, AXES, split_axis=0, concat_axis=0, tiled=True)  7.3 us
    pallas_call x1, Pallas kernels, on_device(): pl.pallas_call(functools.partial(gather_kernel, chunk=4), in_specs=[vmem,...  4.31 us
  transfers between devices with their start and end apart: 9, of which 7 were waited for; matrix products, arithmetic and copies ran while one was open for 2% of the time, Pallas kernels for 17%

profile of v7, /device:TPU:0, one launch (start us, length us, event | category | flops | bytes accessed | tf_op | source)
XLA Modules:
  0.0 90.6 jit_solution(5770317644158437775)
XLA Ops:
  1.3 0.9 %concatenate.3 = f32[8,4096]{1,0:T(8,128)S(1)} pad(f32[7,4096]{1,0:T(8,128)} %param.10, f32[]{:T(128)} %bitcast), padding=0_1x0_0 | pad | bytes 245764 | tf_op jit(solution)/shard_map/concatenate | solution.py:341
  2.4 0.8 copy.16
  3.2 7.3 %all-to-all-start = ((f32[32,8,128]{2,1,0:T(8,128)}), f32[32,8,128]{2,1,0:T(8,128)S(1)}, u32[]{:S(2)}, u32[]{:S(2)}) async-start(f32[32,8,128]{2,1,0:T(8,128)} %bitcast.1.rows_ref), calls=%async_computation | async-start | bytes 262144 | tf_op jit(solution)/shard_map/all_to_all | solution.py:343
  10.5 0.8 reshape.41
  11.4 4.3 %gather_rows.1 = f32[32,16,128]{2,1,0:T(8,128)} custom-call(f32[16,8192]{1,0:T(8,128)} %cell_ref.1, s32[32,1,128]{2,1,0:T(1,128)S(1)} %bitcast.7, f32[32,8,128]{2,1,0:T(8,128)} %bitcast.1.rows_ref), custom_call_target="tpu_custom_call" | custom-call | tf_op jit(solution)/shard_map/gather_rows/pallas_call | solution.py:345
  15.7 2.6 %all-to-all-done.came_ref = f32[32,8,128]{2,1,0:T(8,128)S(1)} async-done(((f32[32,8,128]{2,1,0:T(8,128)}), f32[32,8,128]{2,1,0:T(8,128)S(1)}, u32[]{:S(2)}, u32[]{:S(2)}) %all-to-all-start) | async-done | bytes 131104 | tf_op jit(solution)/shard_map/all_to_all | solution.py:343
  18.3 3.3 %all-to-all-start.1 = ((f32[32,16,128]{2,1,0:T(8,128)}), f32[32,16,128]{2,1,0:T(8,128)S(1)}, u32[]{:S(2)}, u32[]{:S(2)}) async-start(f32[32,16,128]{2,1,0:T(8,128)} %gather_rows.1), calls=%async_computation.1 | async-start | bytes 524288 | tf_op jit(solution)/shard_map/all_to_all | solution.py:353
  22.1 11.0 %phases.1 = (bf16[4,4,1024,256]{3,2,1,0:T(8,128)(2,1)}, bf16[4,4,1024,256]{3,2,1,0:T(8,128)(2,1)}, f32[8,1024]{1,0:T(8,128)}, bf16[1024,128]{1,0:T(8,128)(2,1)}) custom-call(s32[2,32]{1,0:T(2,128)S(1)} %convert_element_type.12.ends_ref, f32[4]{0:T(128)} %wave_ref.5, f32[32,8,128]{2,1,0:T(8,128)S(1)} %all-to-all-done.came_ref, ...), custom_call_target="tpu_custom_call" | custom-call | tf_op jit(solution)/shard_map/phases/pallas_call | solution.py:367
  33.1 0.7 copy-done.1
  33.8 11.7 %radiate.1 = (bf16[8,4,1024,256]{3,2,1,0:T(8,128)(2,1)S(1)}, bf16[8,4,1024,256]{3,2,1,0:T(8,128)(2,1)S(1)}, f32[8,2048]{1,0:T(8,128)S(1)}) custom-call(s32[2,32]{1,0:T(2,128)} %copy-done, f32[4]{0:T(128)} %wave_ref.5, f32[32,16,128]{2,1,0:T(8,128)} %copy-done.1, f32[8,1024]{1,0:T(8,128)} %get-tuple-element.13.rows_ref, ...), custom_call_target="tpu_custom_call" | custom-call | tf_op jit(solution)/shard_map/radiate/pallas_call | solution.py:383
  45.5 0.3 collective-permute-start
  45.9 1.0 %collective-permute-done = f32[8,2048]{1,0:T(8,128)S(1)} collective-permute-done((f32[8,2048]{1,0:T(8,128)S(1)}, f32[8,2048]{1,0:T(8,128)S(1)}, u32[]{:S(2)}, u32[]{:S(2)}) %collective-permute-start) | collective-permute-done | bytes 65568 | tf_op jit(solution)/shard_map/ppermute | solution.py:318
  46.9 2.7 %collective-permute-start.3 = (f32[8,2048]{1,0:T(8,128)S(1)}, f32[8,2048]{1,0:T(8,128)S(1)}, u32[]{:S(2)}, u32[]{:S(2)}) collective-permute-start(f32[8,2048]{1,0:T(8,128)S(1)} %add.21), channel_id=1, source_target_pairs={{0,17},{1,16},{2,19},{3,18},{4,21},{5,20},{6,23},{7,22},{8,25},{9,... | collective-permute-start | bytes 196616 | tf_op jit(solution)/shard_map/ppermute | solution.py:318
  49.6 0.6 collective-permute-start.2
  50.4 1.7 %collective-permute-done.3 = f32[8,2048]{1,0:T(8,128)S(1)} collective-permute-done((f32[8,2048]{1,0:T(8,128)S(1)}, f32[8,2048]{1,0:T(8,128)S(1)}, u32[]{:S(2)}, u32[]{:S(2)}) %collective-permute-start.3) | collective-permute-done | bytes 65568 | tf_op jit(solution)/shard_map/ppermute | solution.py:318
  52.1 1.8 %collective-permute-done.2 = f32[8,2048]{1,0:T(8,128)S(1)} collective-permute-done((f32[8,2048]{1,0:T(8,128)S(1)}, f32[8,2048]{1,0:T(8,128)S(1)}, u32[]{:S(2)}, u32[]{:S(2)}) %collective-permute-start.2) | collective-permute-done | bytes 65568 | tf_op jit(solution)/shard_map/ppermute | solution.py:318
  53.9 0.6 collective-permute-done.1
  54.5 3.4 %collective-permute-start.6 = (f32[8,2048]{1,0:T(8,128)S(1)}, f32[8,2048]{1,0:T(8,128)S(1)}, u32[]{:S(2)}, u32[]{:S(2)}) collective-permute-start(f32[8,2048]{1,0:T(8,128)S(1)} %add_add_fusion.rest_0_), channel_id=1, source_target_pairs={{0,6},{1,7},{2,4},{3,5},{4,2},{5,3},{6,0},{7,1},{8,14},{9,15},{10,... | collective-permute-start | bytes 196616 | tf_op jit(solution)/shard_map/ppermute | solution.py:318
  57.9 1.0 %collective-permute-start.4 = (f32[8,2048]{1,0:T(8,128)S(1)}, f32[8,2048]{1,0:T(8,128)S(1)}, u32[]{:S(2)}, u32[]{:S(2)}) collective-permute-start(f32[8,2048]{1,0:T(8,128)S(1)} %add_add_fusion.rest_0_), channel_id=1, source_target_pairs={{0,2},{1,3},{2,0},{3,1},{4,6},{5,7},{6,4},{7,5},{8,10},{9,11},{10,... | collective-permute-start | bytes 196616 | tf_op jit(solution)/shard_map/ppermute | solution.py:318
  58.9 1.8 %collective-permute-done.6.rest_3_ = f32[8,2048]{1,0:T(8,128)S(1)} collective-permute-done((f32[8,2048]{1,0:T(8,128)S(1)}, f32[8,2048]{1,0:T(8,128)S(1)}, u32[]{:S(2)}, u32[]{:S(2)}) %collective-permute-start.6) | collective-permute-done | bytes 65568 | tf_op jit(solution)/shard_map/ppermute | solution.py:318
  60.7 2.3 %collective-permute-done.5.rest_2_ = f32[8,2048]{1,0:T(8,128)S(1)} collective-permute-done((f32[8,2048]{1,0:T(8,128)S(1)}, f32[8,2048]{1,0:T(8,128)S(1)}, u32[]{:S(2)}, u32[]{:S(2)}) %collective-permute-start.5) | collective-permute-done | bytes 65568 | tf_op jit(solution)/shard_map/ppermute | solution.py:318
  63.0 10.9 %adjoint.1 = (bf16[8,4,1024,256]{3,2,1,0:T(8,128)(2,1)S(1)}, bf16[8,4,1024,256]{3,2,1,0:T(8,128)(2,1)S(1)}, f32[32,16,128]{2,1,0:T(8,128)}, f32[1]{0:T(128)}, f32[4,2,2048]{2,1,0:T(2,128)}) custom-call(s32[2,32]{1,0:T(2,128)} %copy-done, f32[4]{0:T(128)} %wave_ref.5, f32[4,2,2048]{2,1,0:T(2,128)} %target_ref.1, ...), custom_call_target="tpu_custom_call", output_to_operand_aliasing={{0}: (6, {}), {1}: (7, {})} | custom-call | tf_op jit(solution)/shard_map/adjoint/pallas_call | solution.py:405
  73.9 14.6 %all_to_all.15.value_ref = f32[32,16,128]{2,1,0:T(8,128)S(1)} all-to-all(f32[32,16,128]{2,1,0:T(8,128)} %get-tuple-element.22), channel_id=1, replica_groups=mesh['gx'=4,'gy'=8] {'gx','gy'}, dimensions={0} | all-to-all | bytes 524288 | tf_op jit(solution)/shard_map/all_to_all | solution.py:422
  88.5 2.1 %scatter_rows.1 = f32[16,8192]{1,0:T(8,128)} custom-call(f32[32,16,128]{2,1,0:T(8,128)S(1)} %all_to_all.15.value_ref, s32[32,1,128]{2,1,0:T(1,128)S(1)} %bitcast.8), custom_call_target="tpu_custom_call" | custom-call | tf_op jit(solution)/shard_map/scatter_rows/pallas_call | solution.py:423
  (17 shorter events, 1.0 us)
Async XLA Ops:
  3.2 15.0 %all-to-all-start = ((f32[32,8,128]{2,1,0:T(8,128)}), f32[32,8,128]{2,1,0:T(8,128)S(1)}, u32[]{:S(2)}, u32[]{:S(2)}) async-start(f32[32,8,128]{2,1,0:T(8,128)} %bitcast.1.rows_ref), calls=%async_computation | async-start | bytes 262144 | tf_op jit(solution)/shard_map/all_to_all | solution.py:343
  18.3 14.8 %all-to-all-start.1 = ((f32[32,16,128]{2,1,0:T(8,128)}), f32[32,16,128]{2,1,0:T(8,128)S(1)}, u32[]{:S(2)}, u32[]{:S(2)}) async-start(f32[32,16,128]{2,1,0:T(8,128)} %gather_rows.1), calls=%async_computation.1 | async-start | bytes 524288 | tf_op jit(solution)/shard_map/all_to_all | solution.py:353
  22.1 11.0 %copy-start = (s32[2,32]{1,0:T(2,128)}, s32[2,32]{1,0:T(2,128)S(1)}, u32[]{:S(2)}) copy-start(s32[2,32]{1,0:T(2,128)S(1)} %convert_element_type.12.ends_ref) | copy-start | bytes 772
  33.1 0.7 copy-start.1
  45.5 1.3 %collective-permute-start = (f32[8,2048]{1,0:T(8,128)S(1)}, f32[8,2048]{1,0:T(8,128)S(1)}, u32[]{:S(2)}, u32[]{:S(2)}) collective-permute-start(f32[8,2048]{1,0:T(8,128)S(1)} %get-tuple-element.19), channel_id=1, source_target_pairs={{0,8},{1,9},{2,10},{3,11},{4,12},{5,13},{6,14},{7,15},{8,0},{9,1},... | collective-permute-start | bytes 196616 | tf_op jit(solution)/shard_map/ppermute | solution.py:318
  46.9 5.2 %collective-permute-start.3 = (f32[8,2048]{1,0:T(8,128)S(1)}, f32[8,2048]{1,0:T(8,128)S(1)}, u32[]{:S(2)}, u32[]{:S(2)}) collective-permute-start(f32[8,2048]{1,0:T(8,128)S(1)} %add.21), channel_id=1, source_target_pairs={{0,17},{1,16},{2,19},{3,18},{4,21},{5,20},{6,23},{7,22},{8,25},{9,... | collective-permute-start | bytes 196616 | tf_op jit(solution)/shard_map/ppermute | solution.py:318
  49.6 4.3 %collective-permute-start.2 = (f32[8,2048]{1,0:T(8,128)S(1)}, f32[8,2048]{1,0:T(8,128)S(1)}, u32[]{:S(2)}, u32[]{:S(2)}) collective-permute-start(f32[8,2048]{1,0:T(8,128)S(1)} %add.21), channel_id=1, source_target_pairs={{0,16},{1,17},{2,18},{3,19},{4,20},{5,21},{6,22},{7,23},{8,24},{9,... | collective-permute-start | bytes 196616 | tf_op jit(solution)/shard_map/ppermute | solution.py:318
  50.2 4.3 %collective-permute-start.1 = (f32[8,2048]{1,0:T(8,128)S(1)}, f32[8,2048]{1,0:T(8,128)S(1)}, u32[]{:S(2)}, u32[]{:S(2)}) collective-permute-start(f32[8,2048]{1,0:T(8,128)S(1)} %add.21), channel_id=1, source_target_pairs={{0,1},{1,0},{2,3},{3,2},{4,5},{5,4},{6,7},{7,6},{8,9},{9,8},{10,11... | collective-permute-start | bytes 196616 | tf_op jit(solution)/shard_map/ppermute | solution.py:318
  54.5 6.2 %collective-permute-start.6 = (f32[8,2048]{1,0:T(8,128)S(1)}, f32[8,2048]{1,0:T(8,128)S(1)}, u32[]{:S(2)}, u32[]{:S(2)}) collective-permute-start(f32[8,2048]{1,0:T(8,128)S(1)} %add_add_fusion.rest_0_), channel_id=1, source_target_pairs={{0,6},{1,7},{2,4},{3,5},{4,2},{5,3},{6,0},{7,1},{8,14},{9,15},{10,... | collective-permute-start | bytes 196616 | tf_op jit(solution)/shard_map/ppermute | solution.py:318
  57.9 5.2 %collective-permute-start.5 = (f32[8,2048]{1,0:T(8,128)S(1)}, f32[8,2048]{1,0:T(8,128)S(1)}, u32[]{:S(2)}, u32[]{:S(2)}) collective-permute-start(f32[8,2048]{1,0:T(8,128)S(1)} %add_add_fusion.rest_0_), channel_id=1, source_target_pairs={{0,4},{1,5},{2,6},{3,7},{4,0},{5,1},{6,2},{7,3},{8,12},{9,13},{10,... | collective-permute-start | bytes 196616 | tf_op jit(solution)/shard_map/ppermute | solution.py:318
  57.9 5.2 %collective-permute-start.4 = (f32[8,2048]{1,0:T(8,128)S(1)}, f32[8,2048]{1,0:T(8,128)S(1)}, u32[]{:S(2)}, u32[]{:S(2)}) collective-permute-start(f32[8,2048]{1,0:T(8,128)S(1)} %add_add_fusion.rest_0_), channel_id=1, source_target_pairs={{0,2},{1,3},{2,0},{3,1},{4,6},{5,7},{6,4},{7,5},{8,10},{9,11},{10,... | collective-permute-start | bytes 196616 | tf_op jit(solution)/shard_map/ppermute | solution.py:318
